TPU v7x, 512 devices: a whole 4x8x8 slice. The times are simulated.
512 devices in a mesh: view: 2 (over z_hi), dp: 32 (over x, y), mp: 8 (over z_lo, core).
Axes of the slice: x: 4, y: 8, z: 8 (z_hi: 2, z_lo: 4; z = z_hi * 4 + z_lo), core: 2. Of those that a mesh axis runs over, the one named last changes fastest.
Arguments:
- views: bfloat16 [2, 32768, 768], P('view', ('dp', 'mp')), may hold values from -1 to 1
- prototypes: bfloat16 [768, 4096], P(None, 'mp'), may hold values from -1 to 1
Outputs:
- view_grad: bfloat16 [2, 32768, 768], P('view', ('dp', 'mp'))
- proto_grad: float32 [768, 4096], P(('view', 'dp'), 'mp')
All inputs are finite; a program needn't handle non-finite values.
Results may differ from a plain program's by a relative error of at most 0.019.
Values may be sent and summed in bfloat16 or wider, within the bound.
No kernel may reach another device: no remote copies, remote signals or barrier semaphores. Data moves between devices by JAX's collectives and lax.ppermute only.
A program may use at most 64 MiB of HBM per device.

v0:
```python
import jax
import jax.numpy as jnp
from jax import lax
from jax.sharding import PartitionSpec as P

SWEEPS = 3


sink_eps = 0.05
pred_temp = 0.1
grad_scale = 8.0


def swapped(value, axis, stride):
    mask = 2**stride
    pairs = [(source, source ^ mask) for source in range(lax.axis_size(axis))]
    return lax.ppermute(value, axis, pairs)


def balance_codes(scores):
    expos = jnp.exp(scores / sink_eps)
    for sweep in range(SWEEPS):
        column_total = lax.psum(jnp.sum(expos, axis=1), "dp")
        expos = expos / column_total[:, None, :]
        row_total = lax.psum(jnp.sum(expos, axis=2), "mp")
        expos = expos / row_total[:, :, None]
    return expos


def on_device(views, prototypes):
    inputs = views.astype(jnp.float32)
    row_norm = jnp.sqrt(jnp.sum(inputs * inputs, axis=-1, keepdims=True) + 1e-06)
    unit_rows = inputs / row_norm
    unit_half = unit_rows.astype(jnp.bfloat16)
    weights = prototypes.astype(jnp.float32)
    proto_norm = jnp.sqrt(jnp.sum(weights * weights, axis=0, keepdims=True) + 1e-06)
    columns = weights / proto_norm
    columns_half = columns.astype(jnp.bfloat16)
    grouped = lax.all_gather(unit_half, "mp", axis=1, tiled=True)
    scores = jnp.einsum("vrd,dk->vrk", grouped, columns_half, preferred_element_type=jnp.float32)
    balanced = balance_codes(scores)
    partner_codes = swapped(balanced[0].astype(jnp.bfloat16), "view", 0)
    expo_pred = jnp.exp(scores[0] / pred_temp)
    pred_total = lax.psum(jnp.sum(expo_pred, axis=1), "mp")
    predicted = expo_pred / pred_total[:, None]
    grad_half = (grad_scale * (predicted - partner_codes.astype(jnp.float32)) / pred_temp).astype(
        jnp.bfloat16
    )
    page_grad = lax.psum_scatter(
        lax.dot_general(
            grad_half, columns_half, (((1,), (1,)), ((), ())), preferred_element_type=jnp.float32
        ).astype(jnp.bfloat16),
        "mp",
        scatter_dimension=0,
        tiled=True,
    ).astype(jnp.float32)
    own_unit = unit_rows[0]
    inner_rows = jnp.sum(own_unit * page_grad, axis=-1, keepdims=True)
    view_grad = ((page_grad - own_unit * inner_rows) / row_norm[0]).astype(jnp.bfloat16)[None]
    group_unit = grouped[0]
    share_rows = prototypes.shape[0] // (lax.axis_size("view") * lax.axis_size("dp"))
    share_start = lax.axis_index(("view", "dp")) * share_rows
    column_grad = lax.dot_general(
        group_unit, grad_half, (((0,), (0,)), ((), ())), preferred_element_type=jnp.float32
    )
    column_total = lax.psum(column_grad, ("view", "dp"))
    inner_cols = jnp.sum(columns * column_total, axis=0, keepdims=True)
    proto_full = (column_total - columns * inner_cols) / proto_norm
    proto_grad = lax.dynamic_slice_in_dim(proto_full, share_start, share_rows, 0)
    return (view_grad, proto_grad)


def solution(mesh):
    placed = (P("view", ("dp", "mp"), None), P(None, "mp"))
    return jax.shard_map(
        on_device,
        mesh=mesh,
        in_specs=placed,
        out_specs=(P("view", ("dp", "mp"), None), P(("view", "dp"), "mp")),
        check_vma=False,
    )
```

profile of v0, /device:TPU:6, one launch (start us, length us, event | category | flops | bytes accessed | tf_op | source)
XLA Modules:
  0.0 1263.3 jit_solution(8876925585181075166)
XLA Ops:
  7.2 0.0 all-gather.2.cloned.1.call-start
  7.2 1.0 fusion.19
  8.3 1.7 fusion.27
  10.0 0.0 all-gather.2.cloned.1.call-update
  10.0 0.0 all-reduce.3.cloned.1.call-start
  10.1 1.3 fusion.13
  11.4 45.1 %all-gather.2.cloned.1.call-done = bf16[1,1024,768]{2,1,0:T(8,128)(2,1)} async-done(((bf16[1,128,768]{2,1,0:T(8,128)(2,1)}), bf16[1,1024,768]{2,1,0:T(8,128)(2,1)}) %all-gather.2.cloned.1.call-update) | async-done | bytes 1572880 | tf_op jit(solution)/shard_map/all_gather | solution.py:39
  56.5 2.7 fusion.18
  59.3 63.0 %psum.57 = f32[512]{0:T(512)S(1)} all-reduce(f32[512]{0:T(512)S(1)} %get-tuple-element.8), channel_id=1, replica_groups=mesh['view'=2,'dp'=32,'mp'=8] {'dp'}, use_global_device_ids=true, to_apply=%region_5.0 | all-reduce | flops 512 | bytes 4096 | tf_op jit(solution)/shard_map/psum | solution.py:23
  122.2 0.7 fusion.12
  122.9 13.6 %psum.58 = f32[1024]{0:T(1024)S(1)} all-reduce(f32[1024]{0:T(1024)S(1)} %get-tuple-element.3), channel_id=1, replica_groups=mesh['view'=2,'dp'=32,'mp'=8] {'mp'}, use_global_device_ids=true, to_apply=%region_7.0 | all-reduce | flops 1024 | bytes 8192 | tf_op jit(solution)/shard_map/psum | solution.py:25
  136.5 0.7 fusion.8
  137.3 68.9 %psum.59 = f32[512]{0:T(512)S(1)} all-reduce(f32[512]{0:T(512)S(1)} %fusion.8), channel_id=1, replica_groups=mesh['view'=2,'dp'=32,'mp'=8] {'dp'}, use_global_device_ids=true, to_apply=%region_9.0 | all-reduce | flops 512 | bytes 4096 | tf_op jit(solution)/shard_map/psum | solution.py:23
  206.1 0.6 fusion.9
  206.7 13.6 %psum.60 = f32[1024]{0:T(1024)S(1)} all-reduce(f32[1024]{0:T(1024)S(1)} %fusion.9), channel_id=1, replica_groups=mesh['view'=2,'dp'=32,'mp'=8] {'mp'}, use_global_device_ids=true, to_apply=%region_11.0 | all-reduce | flops 1024 | bytes 8192 | tf_op jit(solution)/shard_map/psum | solution.py:25
  220.3 0.8 fusion.10
  221.2 70.7 %psum.61 = f32[512]{0:T(512)S(1)} all-reduce(f32[512]{0:T(512)S(1)} %fusion.10), channel_id=1, replica_groups=mesh['view'=2,'dp'=32,'mp'=8] {'dp'}, use_global_device_ids=true, to_apply=%region_13.0 | all-reduce | flops 512 | bytes 4096 | tf_op jit(solution)/shard_map/psum | solution.py:23
  291.9 0.7 fusion.11
  292.6 13.9 %all-reduce = (f32[1024]{0:T(1024)S(1)}, f32[1024]{0:T(1024)S(1)}) all-reduce(f32[1024]{0:T(1024)S(1)} %fusion.11, f32[1024]{0:T(1024)S(1)} %get-tuple-element.2), channel_id=1, replica_groups=mesh['view'=2,'dp'=32,'mp'=8] {'mp'}, use_global_device_ids=true, to_apply=%region_15.0 | all-reduce | flops 2048 | bytes 16384 | tf_op jit(solution)/shard_map/psum | solution.py:25
  306.5 0.8 fusion.7
  307.4 5.8 collective-permute-start
  313.2 44.7 %collective-permute-done = bf16[1024,512]{0,1:T(8,128)(2,1)S(1)} collective-permute-done((bf16[1024,512]{0,1:T(8,128)(2,1)S(1)}, bf16[1024,512]{0,1:T(8,128)(2,1)S(1)}, u32[]{:S(2)}, u32[]{:S(2)}) %collective-permute-start) | collective-permute-done | bytes 1048608 | tf_op jit(solution)/shard_map/ppermute | solution.py:17
  358.0 0.0 copy-start.2
  358.0 0.6 multiply_convert_fusion
  358.5 0.8 copy-done.2
  359.4 0.0 copy-start.1
  359.4 2.2 fusion.14
  361.6 0.0 all-reduce.3.cloned.1.call-update
  361.6 0.0 reduce-scatter.2.cloned.1.call-start
  361.6 0.0 copy-done.1
  361.6 2.2 convolution_convert_fusion
  363.8 0.0 reduce-scatter.2.cloned.1.call-update
  363.9 0.0 copy-start
  363.9 824.8 %all-reduce.3.cloned.1.call-done = f32[768,512]{1,0:T(8,128)} async-done(((f32[768,512]{1,0:T(8,128)}), f32[768,512]{1,0:T(8,128)}) %all-reduce.3.cloned.1.call-update) | async-done | bytes 1572880 | tf_op jit(solution)/shard_map/psum | solution.py:66
  1188.7 1.7 multiply_reduce_fusion
  1190.5 1.4 fusion.26
  1191.9 61.9 %reduce-scatter.2.cloned.1.call-done = bf16[128,768]{1,0:T(8,128)(2,1)} async-done(((bf16[1024,768]{1,0:T(8,128)(2,1)}), bf16[128,768]{1,0:T(8,128)(2,1)}) %reduce-scatter.2.cloned.1.call-update) | async-done | bytes 196624 | tf_op jit(solution)/shard_map/reduce_scatter | solution.py:49
  1253.8 0.0 copy-done
  1253.8 1.2 fusion.20
  1254.9 1.8 fusion.25
  (2 shorter events, 0.0 us)
Async XLA Ops:
  7.2 49.4 %all-gather.2.cloned.1.call-start = ((), (), s32[]{:S(2)}) async-start(), calls=%async_computation.1 | async-start | bytes 1769472 | tf_op jit(solution)/shard_map/all_gather | solution.py:39
  10.0 1178.7 %all-reduce.3.cloned.1.call-start = ((), (), s32[]{:S(2)}) async-start(), calls=%async_computation.3 | async-start | bytes 3145728 | tf_op jit(solution)/shard_map/psum | solution.py:66
  307.4 50.6 %collective-permute-start = (bf16[1024,512]{0,1:T(8,128)(2,1)S(1)}, bf16[1024,512]{0,1:T(8,128)(2,1)S(1)}, u32[]{:S(2)}, u32[]{:S(2)}) collective-permute-start(bf16[1024,512]{0,1:T(8,128)(2,1)S(1)} %fusion.7), channel_id=1, source_target_pairs={{0,256},{256,0},{1,257},{257,1},{2,258},{258,2},{3,259},{259,3},{4... | collective-permute-start | bytes 3145736 | tf_op jit(solution)/shard_map/ppermute | solution.py:17
  358.0 1.4 copy-start.2
  359.4 2.3 copy-start.1
  361.6 892.2 %reduce-scatter.2.cloned.1.call-start = ((), (), s32[]{:S(2)}) async-start(), calls=%async_computation.2 | async-start | bytes 1769472 | tf_op jit(solution)/shard_map/reduce_scatter | solution.py:49
  363.9 889.9 %copy-start = (bf16[1,128,768]{2,1,0:T(8,128)(2,1)S(1)}, bf16[1,128,768]{2,1,0:T(8,128)(2,1)}, u32[]{:S(2)}) copy-start(bf16[1,128,768]{2,1,0:T(8,128)(2,1)} %param.2) | copy-start | bytes 589828
Sparse Core Ops, SparseCore 0:
  10.7 45.8 all-gather.1
  361.7 826.9 all-reduce.2
  1191.8 61.9 reduce-scatter.1
where the time goes:
time: 1260 us
  waiting for transfers between devices  977 us (78%)
  blocking collectives  244 us (19%)
  other arithmetic  15.2 us (1%)
  between operations  13.8 us (1%)
    psum x1, waiting for transfers between devices, on_device(): column_total = lax.psum(column_grad, ('view', 'dp'))  825 us
    psum x3, blocking collectives, balance_codes(): column_total = lax.psum(jnp.sum(expos, axis=1), 'dp')  203 us
    reduce_scatter x1, waiting for transfers between devices, on_device(): lax.psum_scatter(lax.dot_general(grad_half, columns_half, (((1,), (1,)),...  61.9 us
    all_gather x1, waiting for transfers between devices, on_device(): grouped = lax.all_gather(unit_half, 'mp', axis=1, tiled=True)  45.1 us
    ppermute x1, waiting for transfers between devices, swapped(): return lax.ppermute(value, axis, pairs)  44.7 us
    psum x3, blocking collectives, balance_codes(): row_total = lax.psum(jnp.sum(expos, axis=2), 'mp')  41.1 us
  transfers between devices with their start and end apart: 4, of which 4 were waited for; matrix products, arithmetic and copies ran while one was open for 1% of the time, Pallas kernels for 0%

commit v1 on v0

v1 whole, which is shorter than its diff:
```python
import jax
import jax.numpy as jnp
from jax import lax
from jax.sharding import Mesh
from jax.sharding import PartitionSpec as P

SWEEPS = 3

sink_eps = 0.05
pred_temp = 0.1
grad_scale = 8.0

FINE = ("zh", "x", "y", "zl", "core")
DP = ("x", "y")
MP = ("zl", "core")


def swapped(value, axis):
    return lax.ppermute(value, axis, [(0, 1), (1, 0)])


def shared(vector, axes):
    size = lax.axis_size(axes)
    spread = jnp.broadcast_to(vector[None], (size,) + vector.shape)
    return lax.all_to_all(spread, axes, 0, 0, tiled=True)


def on_device(views, prototypes):
    f32, bf16 = jnp.float32, jnp.bfloat16
    inputs = views[0].astype(f32)
    row_norm = jnp.sqrt(jnp.sum(inputs * inputs, axis=-1, keepdims=True) + 1e-06)
    unit_rows = inputs / row_norm
    unit_half = unit_rows.astype(bf16)
    weights = prototypes.astype(f32)
    proto_norm = jnp.sqrt(jnp.sum(weights * weights, axis=0, keepdims=True) + 1e-06)
    columns = weights / proto_norm
    columns_half = columns.astype(bf16)

    rows, width = unit_half.shape
    protos = columns_half.shape[1]
    line = lax.all_gather(unit_half, "zl", axis=0, tiled=False)
    other = swapped(line, "core")
    core = lax.axis_index("core")
    first = jnp.where(core == 0, line, other)
    second = jnp.where(core == 0, other, line)
    grouped = jnp.stack([first, second], axis=1).reshape(-1, width)
    group_rows = grouped.shape[0]

    scores = jnp.dot(grouped, columns_half, preferred_element_type=f32)
    expos = jnp.exp(scores / sink_eps)
    expos, expos_sent = lax.optimization_barrier((expos, expos.astype(bf16)))
    partner_expos = swapped(expos_sent, "zh")
    expo_pred = jnp.exp(scores / pred_temp)

    row_scale = jnp.ones((group_rows,), f32)
    for sweep in range(SWEEPS):
        partial = jnp.sum(expos * row_scale[:, None], axis=0)
        col_scale = 1.0 / jnp.sum(shared(partial, DP), axis=0)
        partial = jnp.sum(expos * col_scale[None, :], axis=1)
        if sweep == 0:
            both = jnp.concatenate([partial, jnp.sum(expo_pred, axis=1)])
            totals = jnp.sum(shared(both, MP), axis=0)
            row_scale = 1.0 / totals[:group_rows]
            pred_total = totals[group_rows:]
        elif sweep < SWEEPS - 1:
            row_scale = 1.0 / jnp.sum(shared(partial, MP), axis=0)
        else:
            partner_cols = swapped(col_scale, "zh")
            mp_size = lax.axis_size(MP)
            pieces = shared(partial, ("zh",) + MP).reshape(2, mp_size, group_rows)
            totals = jnp.sum(pieces, axis=1)
            me = lax.axis_index("zh")
            partner_rows = 1.0 / jnp.where(me == 0, totals[1], totals[0])

    codes = (partner_expos.astype(f32) * partner_cols[None, :] * partner_rows[:, None]).astype(bf16)
    predicted = expo_pred / pred_total[:, None]
    grad_half = (grad_scale * (predicted - codes.astype(f32)) / pred_temp).astype(bf16)

    page_part = lax.dot_general(
        grad_half, columns_half, (((1,), (1,)), ((), ())), preferred_element_type=f32
    ).astype(bf16)
    page_grad = lax.psum_scatter(page_part, MP, scatter_dimension=0, tiled=True).astype(f32)

    column_part = lax.dot_general(
        grouped, grad_half, (((0,), (0,)), ((), ())), preferred_element_type=f32
    )
    shares = lax.axis_size("zh") * lax.axis_size(DP)
    share_rows = width // shares
    column_sent = column_part.astype(bf16)
    inner_part = jnp.sum(columns * column_sent.astype(f32), axis=0)
    inner_high = inner_part.astype(bf16)
    inner_low = (inner_part - inner_high.astype(f32)).astype(bf16)
    inner_rows = jnp.broadcast_to(jnp.stack([inner_high, inner_low])[None], (shares, 2, protos))
    parcels = jnp.concatenate([column_sent.reshape(shares, share_rows, protos), inner_rows], axis=1)
    arrived = lax.all_to_all(parcels, ("zh",) + DP, 0, 0, tiled=True)
    summed = jnp.sum(arrived.astype(f32), axis=0)
    column_grad = summed[:share_rows]
    inner_cols = summed[share_rows] + summed[share_rows + 1]
    start = lax.axis_index(("zh",) + DP) * share_rows
    own_columns = lax.dynamic_slice_in_dim(columns, start, share_rows, 0)
    proto_grad = (column_grad - own_columns * inner_cols[None, :]) / proto_norm

    inner = jnp.sum(unit_rows * page_grad, axis=-1, keepdims=True)
    view_grad = ((page_grad - unit_rows * inner) / row_norm).astype(bf16)[None]
    return (view_grad, proto_grad)


def solution(mesh):
    fine = Mesh(mesh.devices.reshape(2, 4, 8, 4, 2), FINE)
    return jax.shard_map(
        on_device,
        mesh=fine,
        in_specs=(P("zh", DP + MP, None), P(None, MP)),
        out_specs=(P("zh", DP + MP, None), P(("zh",) + DP, MP)),
        check_vma=False,
    )
```

time: 1260 us -> 219 us (0.17)
  waiting for transfers between devices: 977 us -> 65.3 us
  blocking collectives: 244 us -> 75.5 us
  starting transfers between devices: 5.96 us -> 35.6 us
    psum x1 -> x0, waiting for transfers between devices: 825 us -> none  [on_device(): column_total = lax.psum(column_grad, ('view', 'dp'))]
    psum x6 -> x0, blocking collectives: 244 us -> none  [the longest x3 203 us: balance_codes(): column_total = lax.psum(jnp.sum(expos, axis=1), 'dp')]
    all_to_all x0 -> x3, waiting for transfers between devices: none -> 55 us  [the longest x1 33.1 us: on_device(): arrived = lax.all_to_all(parcels, ('zh',) + DP, 0, 0, tiled=True)]
    reduce_scatter x1, waiting for transfers between devices: 61.9 us -> 8.11 us  [on_device(): lax.psum_scatter(page_part, MP, scatter_dimension=0, tiled=True).astype(f32)]
    all_to_all x0 -> x4, blocking collectives: none -> 53.2 us  [shared(): return lax.all_to_all(spread, axes, 0, 0, tiled=True)]
    all_gather x1 -> x0, waiting for transfers between devices: 45.1 us -> none  [on_device(): grouped = lax.all_gather(unit_half, 'mp', axis=1, tiled=True)]
    ppermute x1 -> x3, waiting for transfers between devices: 44.7 us -> 2.15 us  [swapped(): return lax.ppermute(value, axis, [(0, 1), (1, 0)])]
    all_gather x0 -> x1, blocking collectives: none -> 22.2 us  [on_device(): line = lax.all_gather(unit_half, 'zl', axis=0, tiled=False)]
  transfers between devices with their start and end apart: 4 -> 7, of which waited for: 4 -> 4; matrix products, arithmetic and copies ran while one was open for 1% -> 4% of each run, Pallas kernels for 0% -> 0%
where the time goes in v1:
time: 219 us; the launch traced here: 216 us
  blocking collectives  75.5 us (34%)
  waiting for transfers between devices  65.3 us (30%)
  starting transfers between devices  35.6 us (16%)
  between operations  14.3 us (7%)
  other arithmetic  13.7 us (6%)
  matrix products  8.53 us (4%)
  local copies, waits for them, and re-layouts  2.67 us (1%)
    all_to_all x4, blocking collectives, shared(): return lax.all_to_all(spread, axes, 0, 0, tiled=True)  53.2 us
    all_to_all x1, waiting for transfers between devices, on_device(): arrived = lax.all_to_all(parcels, ('zh',) + DP, 0, 0, tiled=True)  33.1 us
    all_gather x1, blocking collectives, on_device(): line = lax.all_gather(unit_half, 'zl', axis=0, tiled=False)  22.2 us
    all_to_all x2, waiting for transfers between devices, shared(): return lax.all_to_all(spread, axes, 0, 0, tiled=True)  22 us
    ppermute x3, starting transfers between devices, swapped(): return lax.ppermute(value, axis, [(0, 1), (1, 0)])  17.8 us
    all_to_all x1, starting transfers between devices, on_device(): arrived = lax.all_to_all(parcels, ('zh',) + DP, 0, 0, tiled=True)  9.34 us
    all_to_all x2, starting transfers between devices, shared(): return lax.all_to_all(spread, axes, 0, 0, tiled=True)  8.44 us
    reduce_scatter x1, waiting for transfers between devices, on_device(): lax.psum_scatter(page_part, MP, scatter_dimension=0, tiled=True).astype(f32)  8.11 us
  transfers between devices with their start and end apart: 7, of which 4 were waited for; matrix products, arithmetic and copies ran while one was open for 4% of the time, Pallas kernels for 0%

profile of v1, /device:TPU:6, one launch (start us, length us, event | category | flops | bytes accessed | tf_op | source)
XLA Modules:
  0.0 215.6 jit_solution(13322460763503346803)
XLA Ops:
  7.2 0.0 copy-start.4
  7.2 1.1 fusion.4
  8.3 1.0 fusion.5
  9.3 22.2 %all_gather.4 = bf16[4,128,768]{2,1,0:T(8,128)(2,1)S(1)} all-gather(bf16[1,128,768]{2,1,0:T(8,128)(2,1)S(1)} %fusion.5), channel_id=1, replica_groups=mesh['zh'=2,'x'=4,'y'=8,'zl'=4,'core'=2] {'zl'}, dimensions={0}, use_global_device_ids=true | all-gather | bytes 983040 | tf_op jit(solution)/shard_map/all_gather | solution.py:41
  31.6 1.9 collective-permute-start
  33.5 0.2 fusion.1
  33.7 2.1 collective-permute-done
  35.9 1.2 select_bitcast_fusion.1
  37.1 0.1 pad_maximum_fusion
  37.3 2.9 %fusion = (f32[1024]{0:T(1024)S(1)}, bf16[1024,512]{0,1:T(8,128)(2,1)}, f32[1024,512]{0,1:T(8,128)S(1)}, f32[1024,512]{0,1:T(8,128)}) fusion(bf16[1024,768]{1,0:T(8,128)(2,1)S(1)} %bitcast.32, f32[512]{0:T(512)S(1)} %add_sqrt_fusion, bf16[768,512]{1,0:T(8,128)(2,1)S(1)} %copy-done.4), kind=kOutput, calls=%fused_computation.12 | convolution fusion | flops 808582144 | bytes 7608320 | tf_op jit(solution)/shard_map/dot_general | solution.py:49
  40.2 0.2 reduce_sum.166
  40.5 18.2 %all_to_all.41 = f32[32,1,512]{2,1,0:T(1,128)S(1)} all-to-all(f32[32,1,512]{2,1,0:T(1,128)S(1)} %broadcast_in_dim.16), channel_id=1, replica_groups=mesh['zh'=2,'x'=4,'y'=8,'zl'=4,'core'=2] {'x','y'}, dimensions={0} | all-to-all | bytes 131072 | tf_op jit(solution)/shard_map/all_to_all | solution.py:25
  58.6 0.1 reduce_sum.167
  58.7 0.2 multiply_reduce_fusion.4
  59.0 8.8 %all_to_all.42 = f32[8,1,2048]{2,1,0:T(1,128)S(1)} all-to-all(f32[8,1,2048]{2,1,0:T(1,128)S(1)} %broadcast_in_dim.17), channel_id=1, replica_groups=mesh['zh'=2,'x'=4,'y'=8,'zl'=4,'core'=2] {'zl','core'}, dimensions={0} | all-to-all | bytes 131072 | tf_op jit(solution)/shard_map/all_to_all | solution.py:25
  67.8 0.1 reduce_sum.170
  67.8 0.2 multiply_reduce_fusion.3
  68.1 13.2 %all_to_all.43 = f32[32,1,512]{2,1,0:T(1,128)S(1)} all-to-all(f32[32,1,512]{2,1,0:T(1,128)S(1)} %broadcast_in_dim.18), channel_id=1, replica_groups=mesh['zh'=2,'x'=4,'y'=8,'zl'=4,'core'=2] {'x','y'}, dimensions={0} | all-to-all | bytes 131072 | tf_op jit(solution)/shard_map/all_to_all | solution.py:25
  81.2 0.1 reduce_sum.172
  81.3 0.2 multiply_reduce_fusion.2
  81.5 0.6 broadcast_in_dim.19
  82.2 3.3 %all-to-all-start.3 = ((f32[8,1,1024]{2,1,0:T(1,128)}), f32[8,1,1024]{2,1,0:T(1,128)S(1)}, u32[]{:S(2)}, u32[]{:S(2)}) async-start(f32[8,1,1024]{2,1,0:T(1,128)} %broadcast_in_dim.19), calls=%async_computation.3 | async-start | bytes 65536 | tf_op jit(solution)/shard_map/all_to_all | solution.py:25
  85.5 8.2 %collective-permute-start.1 = (bf16[1024,512]{0,1:T(8,128)(2,1)}, bf16[1024,512]{0,1:T(8,128)(2,1)S(1)}, u32[]{:S(2)}, u32[]{:S(2)}) collective-permute-start(bf16[1024,512]{0,1:T(8,128)(2,1)} %get-tuple-element.5), channel_id=1, source_target_pairs={{0,256},{256,0},{1,257},{257,1},{2,258},{258,2},{3,259},{259,3},{4... | collective-permute-start | bytes 3145736 | tf_op jit(solution)/shard_map/ppermute | solution.py:19
  93.8 0.2 multiply_reduce_fusion.1
  94.0 13.2 %all_to_all.44 = f32[32,1,512]{2,1,0:T(1,128)S(1)} all-to-all(f32[32,1,512]{2,1,0:T(1,128)S(1)} %broadcast_in_dim.20), channel_id=1, replica_groups=mesh['zh'=2,'x'=4,'y'=8,'zl'=4,'core'=2] {'x','y'}, dimensions={0} | all-to-all | bytes 131072 | tf_op jit(solution)/shard_map/all_to_all | solution.py:25
  107.2 0.1 reduce_sum.176
  107.2 0.2 multiply_reduce_fusion
  107.5 0.7 broadcast_in_dim.21
  108.1 5.1 %all-to-all-start.5 = ((f32[16,1,1024]{2,1,0:T(1,128)}), f32[16,1,1024]{2,1,0:T(1,128)S(1)}, u32[]{:S(2)}, u32[]{:S(2)}) async-start(f32[16,1,1024]{2,1,0:T(1,128)} %broadcast_in_dim.21), calls=%async_computation.5 | async-start | bytes 131072 | tf_op jit(solution)/shard_map/all_to_all | solution.py:25
  113.2 0.0 reduce-scatter.2.cloned.1.call-start
  113.3 7.7 %collective-permute-start.2 = (f32[512]{0:T(512)S(1)}, f32[512]{0:T(512)S(1)}, u32[]{:S(2)}, u32[]{:S(2)}) collective-permute-start(f32[512]{0:T(512)S(1)} %broadcast_divide_fusion.1), channel_id=1, source_target_pairs={{0,256},{256,0},{1,257},{257,1},{2,258},{258,2},{3,259},{259,3},{4... | collective-permute-start | bytes 6152 | tf_op jit(solution)/shard_map/ppermute | solution.py:19
  121.0 22.0 %all-to-all-done.5 = f32[16,1,1024]{2,1,0:T(1,128)S(1)} async-done(((f32[16,1,1024]{2,1,0:T(1,128)}), f32[16,1,1024]{2,1,0:T(1,128)S(1)}, u32[]{:S(2)}, u32[]{:S(2)}) %all-to-all-start.5) | async-done | bytes 65568 | tf_op jit(solution)/shard_map/all_to_all | solution.py:25
  143.1 0.0 copy-start.5
  143.1 2.4 %multiply_convert_fusion = bf16[1024,512]{0,1:T(8,128)(2,1)S(1)} fusion(f32[1024,512]{0,1:T(8,128)} %get-tuple-element.15, bf16[1024,512]{0,1:T(8,128)(2,1)S(1)} %collective-permute-done.1, f32[1024]{0:T(1024)S(1)} %bitcast.34, f32[512]{0:T(512)S(1)} %collective-permute-done.2, f32[1024]{0:T(1024)S(1)} %get-tuple-element.13), kind=kLoop, calls=%fused_computation.1 | loop fusion | flops 5242880 | bytes 4204544 | tf_op jit(solution)/shard_map/convert_element_type | solution.py:77
  145.4 1.0 copy-done.3
  146.4 2.2 %convolution_convert_fusion = bf16[1024,768]{1,0:T(8,128)(2,1)} fusion(bf16[1024,512]{0,1:T(8,128)(2,1)S(1)} %multiply_convert_fusion, bf16[768,512]{1,0:T(8,128)(2,1)S(1)} %copy-done.5, f32[512]{0:T(512)S(1)} %add_sqrt_fusion), kind=kOutput, calls=%fused_computation.13 | convolution fusion | flops 807272448 | bytes 3409920 | tf_op jit(solution)/shard_map/dot_general | solution.py:79
  148.6 0.0 reduce-scatter.2.cloned.1.call-update
  148.6 3.4 %convert_divide_fusion = (f32[768,512]{1,0:T(8,128)}, f32[512]{0:T(512)S(1)}, bf16[768,512]{1,0:T(8,128)(2,1)S(1)}) fusion(bf16[768,512]{1,0:T(8,128)(2,1)S(1)} %copy-done.6, f32[512]{0:T(512)S(1)} %add_sqrt_fusion, bf16[1024,768]{1,0:T(8,128)(2,1)S(1)} %bitcast.33, bf16[1024,512]{0,1:T(8,128)(2,1)} %copy-done.3), kind=kOutput, calls=%fused_computation.10 | convolution fusion | flops 807665152 | bytes 5771264 | tf_op jit(solution)/shard_map/dot_general | solution.py:84
  152.0 0.2 reshape.124
  152.3 0.1 broadcast_in_dim.23
  152.3 1.3 pad_maximum_fusion.1
  153.6 9.3 %all-to-all-start.6 = ((bf16[64,14,512]{2,1,0:T(8,128)(2,1)}), bf16[64,14,512]{2,1,0:T(8,128)(2,1)S(1)}, u32[]{:S(2)}, u32[]{:S(2)}) async-start(bf16[64,14,512]{2,1,0:T(8,128)(2,1)} %pad_maximum_fusion.1), calls=%async_computation.7 | async-start | bytes 2097152 | tf_op jit(solution)/shard_map/all_to_all | solution.py:95
  163.0 33.1 %all-to-all-done.6 = bf16[64,14,512]{2,1,0:T(8,128)(2,1)S(1)} async-done(((bf16[64,14,512]{2,1,0:T(8,128)(2,1)}), bf16[64,14,512]{2,1,0:T(8,128)(2,1)S(1)}, u32[]{:S(2)}, u32[]{:S(2)}) %all-to-all-start.6) | async-done | bytes 917536 | tf_op jit(solution)/shard_map/all_to_all | solution.py:95
  196.1 0.2 convert_reduce_fusion
  196.3 1.4 fusion.13
  197.7 8.1 %reduce-scatter.2.cloned.1.call-done = bf16[128,768]{1,0:T(8,128)(2,1)} async-done(((bf16[1024,768]{1,0:T(8,128)(2,1)}), bf16[128,768]{1,0:T(8,128)(2,1)}) %reduce-scatter.2.cloned.1.call-update) | async-done | bytes 196624 | tf_op jit(solution)/shard_map/reduce_scatter | solution.py:82
  205.8 1.2 fusion.6
  207.0 1.8 fusion.12
  (33 shorter events, 0.3 us)
Async XLA Ops:
  7.2 26.3 %copy-start.4 = (bf16[768,512]{1,0:T(8,128)(2,1)S(1)}, bf16[768,512]{1,0:T(8,128)(2,1)}, u32[]{:S(2)}) copy-start(bf16[768,512]{1,0:T(8,128)(2,1)} %param.3) | copy-start | bytes 2359300
  31.6 4.3 %collective-permute-start = (bf16[4,128,768]{2,1,0:T(8,128)(2,1)S(1)}, bf16[4,128,768]{2,1,0:T(8,128)(2,1)}, u32[]{:S(2)}, u32[]{:S(2)}) collective-permute-start(bf16[4,128,768]{2,1,0:T(8,128)(2,1)S(1)} %all_gather.4), channel_id=1, source_target_pairs={{0,1},{1,0},{2,3},{3,2},{4,5},{5,4},{6,7},{7,6},{8,9},{9,8},{10,11... | collective-permute-start | bytes 2359304 | tf_op jit(solution)/shard_map/ppermute | solution.py:19
  37.3 3.0 %copy-start.1 = (bf16[4,2,128,768]{3,2,1,0:T(8,128)(2,1)}, bf16[4,2,128,768]{3,2,1,0:T(8,128)(2,1)S(1)}, u32[]{:S(2)}) copy-start(bf16[4,2,128,768]{3,2,1,0:T(8,128)(2,1)S(1)} %pad_maximum_fusion) | copy-start | bytes 4718596
  82.2 11.5 %all-to-all-start.3 = ((f32[8,1,1024]{2,1,0:T(1,128)}), f32[8,1,1024]{2,1,0:T(1,128)S(1)}, u32[]{:S(2)}, u32[]{:S(2)}) async-start(f32[8,1,1024]{2,1,0:T(1,128)} %broadcast_in_dim.19), calls=%async_computation.3 | async-start | bytes 65536 | tf_op jit(solution)/shard_map/all_to_all | solution.py:25
  85.5 57.5 %collective-permute-start.1 = (bf16[1024,512]{0,1:T(8,128)(2,1)}, bf16[1024,512]{0,1:T(8,128)(2,1)S(1)}, u32[]{:S(2)}, u32[]{:S(2)}) collective-permute-start(bf16[1024,512]{0,1:T(8,128)(2,1)} %get-tuple-element.5), channel_id=1, source_target_pairs={{0,256},{256,0},{1,257},{257,1},{2,258},{258,2},{3,259},{259,3},{4... | collective-permute-start | bytes 3145736 | tf_op jit(solution)/shard_map/ppermute | solution.py:19
  108.1 34.9 %all-to-all-start.5 = ((f32[16,1,1024]{2,1,0:T(1,128)}), f32[16,1,1024]{2,1,0:T(1,128)S(1)}, u32[]{:S(2)}, u32[]{:S(2)}) async-start(f32[16,1,1024]{2,1,0:T(1,128)} %broadcast_in_dim.21), calls=%async_computation.5 | async-start | bytes 131072 | tf_op jit(solution)/shard_map/all_to_all | solution.py:25
  113.2 92.6 %reduce-scatter.2.cloned.1.call-start = ((), (), s32[]{:S(2)}) async-start(), calls=%async_computation.8 | async-start | bytes 1769472 | tf_op jit(solution)/shard_map/reduce_scatter | solution.py:82
  113.3 29.8 %collective-permute-start.2 = (f32[512]{0:T(512)S(1)}, f32[512]{0:T(512)S(1)}, u32[]{:S(2)}, u32[]{:S(2)}) collective-permute-start(f32[512]{0:T(512)S(1)} %broadcast_divide_fusion.1), channel_id=1, source_target_pairs={{0,256},{256,0},{1,257},{257,1},{2,258},{258,2},{3,259},{259,3},{4... | collective-permute-start | bytes 6152 | tf_op jit(solution)/shard_map/ppermute | solution.py:19
  143.1 3.3 %copy-start.5 = (bf16[768,512]{1,0:T(8,128)(2,1)S(1)}, bf16[768,512]{1,0:T(8,128)(2,1)}, u32[]{:S(2)}) copy-start(bf16[768,512]{1,0:T(8,128)(2,1)} %param.3) | copy-start | bytes 2359300
  145.4 1.0 copy-start.3
  146.4 2.2 %copy-start.2 = (bf16[4,2,128,768]{3,2,1,0:T(8,128)(2,1)S(1)}, bf16[4,2,128,768]{3,2,1,0:T(8,128)(2,1)}, u32[]{:S(2)}) copy-start(bf16[4,2,128,768]{3,2,1,0:T(8,128)(2,1)} %copy-done.1) | copy-start | bytes 4718596
  146.4 2.2 %copy-start.6 = (bf16[768,512]{1,0:T(8,128)(2,1)S(1)}, bf16[768,512]{1,0:T(8,128)(2,1)}, u32[]{:S(2)}) copy-start(bf16[768,512]{1,0:T(8,128)(2,1)} %param.3) | copy-start | bytes 2359300
  153.6 52.2 %copy-start = (bf16[1,128,768]{2,1,0:T(8,128)(2,1)S(1)}, bf16[1,128,768]{2,1,0:T(8,128)(2,1)}, u32[]{:S(2)}) copy-start(bf16[1,128,768]{2,1,0:T(8,128)(2,1)} %param.2) | copy-start | bytes 589828
  153.6 42.4 %all-to-all-start.6 = ((bf16[64,14,512]{2,1,0:T(8,128)(2,1)}), bf16[64,14,512]{2,1,0:T(8,128)(2,1)S(1)}, u32[]{:S(2)}, u32[]{:S(2)}) async-start(bf16[64,14,512]{2,1,0:T(8,128)(2,1)} %pad_maximum_fusion.1), calls=%async_computation.7 | async-start | bytes 2097152 | tf_op jit(solution)/shard_map/all_to_all | solution.py:95
Sparse Core Ops, SparseCore 0:
  148.7 57.0 reduce-scatter.1

commit v2 on v1

v2 whole, which is shorter than its diff:
```python
import jax
import jax.numpy as jnp
from jax import lax
from jax.sharding import Mesh
from jax.sharding import PartitionSpec as P

SWEEPS = 3

sink_eps = 0.05
pred_temp = 0.1
grad_scale = 8.0

FINE = ("zh", "x", "y", "zl", "core")
DP = ("x", "y")
MP = ("zl", "core")
LANES = 128


def swapped(value, axis):
    return lax.ppermute(value, axis, [(0, 1), (1, 0)])


def shared(vector, axes):
    size = lax.axis_size(axes)
    tile = vector.reshape(1, -1, LANES)
    spread = jnp.broadcast_to(tile, (size,) + tile.shape[1:])
    return lax.all_to_all(spread, axes, 0, 0, tiled=True)


def over_mp(pieces):
    by_core = jnp.sum(pieces.reshape((lax.axis_size("zl"), 2, 2, -1)), axis=0)
    first = lax.axis_index("core") == 0
    own = jnp.where(first, by_core[0], by_core[1])
    other = jnp.where(first, by_core[1], by_core[0])
    return own + other[::-1]


def high_low(vector, copies):
    high = vector.astype(jnp.bfloat16)
    low = (vector - high.astype(jnp.float32)).astype(jnp.bfloat16)
    return jnp.broadcast_to(jnp.stack([high, low])[None], (copies, 2) + vector.shape)


def on_device(views, prototypes):
    f32, bf16 = jnp.float32, jnp.bfloat16
    inputs = views[0].astype(f32)
    row_norm = jnp.sqrt(jnp.sum(inputs * inputs, axis=-1, keepdims=True) + 1e-06)
    unit_rows = inputs / row_norm
    unit_half = unit_rows.astype(bf16)
    weights = prototypes.astype(f32)
    proto_norm = jnp.sqrt(jnp.sum(weights * weights, axis=0, keepdims=True) + 1e-06)
    columns = weights / proto_norm
    columns_half = columns.astype(bf16)

    width = unit_half.shape[1]
    protos = columns_half.shape[1]
    partner_half = swapped(unit_half, "zh")
    line = lax.all_gather(unit_half, "zl", axis=0, tiled=True)
    grouped = jnp.concatenate([line, swapped(line, "core")], axis=0)
    group_rows = grouped.shape[0]
    half_rows = group_rows // 2

    scores = jnp.dot(grouped, columns_half, preferred_element_type=f32)
    expos = jnp.exp(scores / sink_eps)
    expo_pred = jnp.exp(scores / pred_temp)
    partner_all = lax.all_gather(partner_half, MP, axis=0, tiled=False)
    core = lax.axis_index("core")
    partner_all = partner_all.reshape((-1, 2) + partner_half.shape)

    row_scale = None
    for sweep in range(SWEEPS):
        weighted = expos if row_scale is None else expos * row_scale[:, None]
        partial = jnp.sum(weighted, axis=0)
        pieces = shared(partial, DP)
        col_scale = 1.0 / jnp.sum(pieces, axis=0).reshape(protos)
        partial = jnp.sum(expos * col_scale[None, :], axis=1)
        if sweep == 0:
            both = jnp.stack([partial.reshape(2, half_rows), jnp.sum(expo_pred, axis=1).reshape(2, half_rows)], axis=1)
            totals = over_mp(shared(both, MP)).reshape(2, 2, half_rows)
            row_scale = 1.0 / totals[:, 0].reshape(group_rows)
            pred_total = totals[:, 1].reshape(group_rows)
        elif sweep < SWEEPS - 1:
            row_scale = 1.0 / over_mp(shared(partial, MP)).reshape(group_rows)
        else:
            sent = jnp.concatenate([partial, col_scale])
            pieces = shared(sent, ("zh",) + MP).reshape(2, lax.axis_size(MP), group_rows + protos)
            pieces = lax.dynamic_index_in_dim(pieces, 1 - lax.axis_index("zh"), 0, keepdims=False)
            partner_rows = 1.0 / over_mp(pieces[:, :group_rows]).reshape(group_rows)
            partner_cols = lax.dynamic_index_in_dim(
                pieces[:, group_rows:], lax.axis_index(MP), 0, keepdims=False
            )

    first = lax.dynamic_index_in_dim(partner_all, core, 1, keepdims=False).reshape(half_rows, width)
    second = lax.dynamic_index_in_dim(partner_all, 1 - core, 1, keepdims=False).reshape(half_rows, width)
    partner_group = jnp.concatenate([first, second], axis=0)
    partner_scores = jnp.dot(partner_group, columns_half, preferred_element_type=f32)
    partner_expos = jnp.exp(partner_scores / sink_eps)
    codes = (partner_expos * partner_cols[None, :] * partner_rows[:, None]).astype(bf16)
    predicted = expo_pred / pred_total[:, None]
    grad_half = (grad_scale * (predicted - codes.astype(f32)) / pred_temp).astype(bf16)

    by_columns = (((1,), (1,)), ((), ()))
    other_part = lax.dot_general(
        grad_half[half_rows:], columns_half, by_columns, preferred_element_type=f32
    ).astype(bf16)
    arrived_part = swapped(other_part, "core")
    own_part = lax.dot_general(
        grad_half[:half_rows], columns_half, by_columns, preferred_element_type=f32
    ).astype(bf16)
    page_part = (own_part.astype(f32) + arrived_part.astype(f32)).astype(bf16)
    page_grad = lax.psum_scatter(page_part, "zl", scatter_dimension=0, tiled=True).astype(f32)

    column_part = lax.dot_general(
        grouped, grad_half, (((0,), (0,)), ((), ())), preferred_element_type=f32
    )
    n_zh, n_x, n_y = lax.axis_size("zh"), lax.axis_size("x"), lax.axis_size("y")
    share = width // (n_zh * n_x * n_y)
    column_sent = column_part.astype(bf16)
    inner_part = jnp.sum(columns * column_sent.astype(f32), axis=0)
    parcels = column_sent.reshape(n_zh, n_x, n_y * share, protos).transpose(1, 0, 2, 3)
    parcels = parcels.reshape(n_x, n_zh * n_y * share, protos)
    parcels = jnp.concatenate([parcels, high_low(inner_part, n_x)], axis=1)
    summed = jnp.sum(lax.all_to_all(parcels, "x", 0, 0, tiled=True).astype(f32), axis=0)
    column_sent, inner_part = summed[: n_zh * n_y * share], jnp.sum(summed[n_zh * n_y * share :], axis=0)
    parcels = column_sent.astype(bf16).reshape(n_zh * n_y, share, protos)
    parcels = jnp.concatenate([parcels, high_low(inner_part, n_zh * n_y)], axis=1)
    summed = jnp.sum(lax.all_to_all(parcels, ("zh", "y"), 0, 0, tiled=True).astype(f32), axis=0)
    column_grad = summed[:share]
    inner_cols = jnp.sum(summed[share:], axis=0, keepdims=True)
    start = lax.axis_index(("zh",) + DP) * share
    own_columns = lax.dynamic_slice_in_dim(columns, start, share, 0)
    proto_grad = (column_grad - own_columns * inner_cols) / proto_norm

    inner = jnp.sum(unit_rows * page_grad, axis=-1, keepdims=True)
    view_grad = ((page_grad - unit_rows * inner) / row_norm).astype(bf16)[None]
    return (view_grad, proto_grad)


def solution(mesh):
    fine = Mesh(mesh.devices.reshape(2, 4, 8, 4, 2), FINE)
    return jax.shard_map(
        on_device,
        mesh=fine,
        in_specs=(P("zh", DP + MP, None), P(None, MP)),
        out_specs=(P("zh", DP + MP, None), P(("zh",) + DP, MP)),
        check_vma=False,
    )
```

time: 219 us -> 186 us (0.85); the launches traced: 216 us -> 185 us
  waiting for transfers between devices: 65.3 us -> 42.4 us
  blocking collectives: 75.5 us -> 64.1 us
  starting transfers between devices: 35.6 us -> 38.2 us
  other arithmetic: 13.7 us -> 11.3 us
  local copies, waits for them, and re-layouts: 2.67 us -> 5.05 us
    all_to_all x1 -> x2, waiting for transfers between devices: 33.1 us -> 21.7 us  [the longest x1 13.5 us: on_device(): lax.all_to_all(parcels, ('zh', 'y'), 0, 0, tiled=True).astype(f32)]
    all_to_all x4 -> x3, blocking collectives: 53.2 us -> 41.9 us  [shared(): return lax.all_to_all(spread, axes, 0, 0, tiled=True)]
    reduce_scatter x1, waiting for transfers between devices: 8.11 us -> 2.41 us  [on_device(): lax.psum_scatter(page_part, 'zl', scatter_dimension=0, tiled=True)]
    all_to_all x2 -> x3, waiting for transfers between devices: 22 us -> 16.3 us  [shared(): return lax.all_to_all(spread, axes, 0, 0, tiled=True)]
    ppermute x3, starting transfers between devices: 17.8 us -> 12.4 us  [swapped(): return lax.ppermute(value, axis, [(0, 1), (1, 0)])]
    all_to_all x2 -> x3, starting transfers between devices: 8.44 us -> 12.6 us  [shared(): return lax.all_to_all(spread, axes, 0, 0, tiled=True)]
    all_to_all x1 -> x2, starting transfers between devices: 9.34 us -> 13.1 us  [the longest x1 7.81 us: on_device(): lax.all_to_all(parcels, ('zh', 'y'), 0, 0, tiled=True).astype(f32)]
    dot_general x1 -> x3, matrix products: 2.19 us -> 5.92 us  [the longest x1 2.83 us: on_device(): lax.dot_general(grad_half[:half_rows], columns_half, by_columns, preferre...]
  transfers between devices with their start and end apart: 7 -> 10, of which waited for: 4 -> 6; matrix products, arithmetic and copies ran while one was open for 4% -> 7% of each run, Pallas kernels for 0% -> 0%
where the time goes in v2:
time: 186 us; the launch traced here: 185 us
  blocking collectives  64.1 us (34%)
  waiting for transfers between devices  42.4 us (23%)
  starting transfers between devices  38.2 us (21%)
  between operations  14.6 us (8%)
  other arithmetic  11.3 us (6%)
  matrix products  9.25 us (5%)
  local copies, waits for them, and re-layouts  5.05 us (3%)
    all_to_all x3, blocking collectives, shared(): return lax.all_to_all(spread, axes, 0, 0, tiled=True)  41.9 us
    all_gather x1, blocking collectives, on_device(): line = lax.all_gather(unit_half, 'zl', axis=0, tiled=True)  22.2 us
    all_to_all x3, waiting for transfers between devices, shared(): return lax.all_to_all(spread, axes, 0, 0, tiled=True)  16.3 us
    all_to_all x1, waiting for transfers between devices, on_device(): lax.all_to_all(parcels, ('zh', 'y'), 0, 0, tiled=True).astype(f32)  13.5 us
    all_to_all x3, starting transfers between devices, shared(): return lax.all_to_all(spread, axes, 0, 0, tiled=True)  12.6 us
    ppermute x3, starting transfers between devices, swapped(): return lax.ppermute(value, axis, [(0, 1), (1, 0)])  12.4 us
    all_to_all x1, waiting for transfers between devices, on_device(): lax.all_to_all(parcels, 'x', 0, 0, tiled=True).astype(f32)  8.17 us
    all_to_all x1, starting transfers between devices, on_device(): lax.all_to_all(parcels, ('zh', 'y'), 0, 0, tiled=True).astype(f32)  7.81 us
  transfers between devices with their start and end apart: 10, of which 6 were waited for; matrix products, arithmetic and copies ran while one was open for 7% of the time, Pallas kernels for 0%

profile of v2, /device:TPU:6, one launch (start us, length us, event | category | flops | bytes accessed | tf_op | source)
XLA Modules:
  0.0 184.8 jit_solution(10883829822962038868)
XLA Ops:
  7.2 1.1 fusion.13
  8.3 1.0 fusion.21
  9.3 22.2 %all_gather.9 = bf16[512,768]{1,0:T(8,128)(2,1)S(1)} all-gather(bf16[128,768]{1,0:T(8,128)(2,1)S(1)} %fusion.21), channel_id=1, replica_groups=mesh['zh'=2,'x'=4,'y'=8,'zl'=4,'core'=2] {'zl'}, dimensions={0}, use_global_device_ids=true | all-gather | bytes 983040 | tf_op jit(solution)/shard_map/all_gather | solution.py:58
  31.6 1.9 %collective-permute-start = (bf16[512,768]{1,0:T(8,128)(2,1)S(1)}, bf16[512,768]{1,0:T(8,128)(2,1)S(1)}, u32[]{:S(2)}, u32[]{:S(2)}) collective-permute-start(bf16[512,768]{1,0:T(8,128)(2,1)S(1)} %all_gather.9), channel_id=1, source_target_pairs={{0,1},{1,0},{2,3},{3,2},{4,5},{5,4},{6,7},{7,6},{8,9},{9,8},{10,11... | collective-permute-start | bytes 2359304 | tf_op jit(solution)/shard_map/ppermute | solution.py:20
  33.5 0.1 constant_dynamic-update-slice_fusion.1
  33.6 0.2 fusion.1
  33.8 2.0 %collective-permute-done = bf16[512,768]{1,0:T(8,128)(2,1)S(1)} collective-permute-done((bf16[512,768]{1,0:T(8,128)(2,1)S(1)}, bf16[512,768]{1,0:T(8,128)(2,1)S(1)}, u32[]{:S(2)}, u32[]{:S(2)}) %collective-permute-start) | collective-permute-done | bytes 786464 | tf_op jit(solution)/shard_map/ppermute | solution.py:20
  35.7 0.1 constant_dynamic-update-slice_fusion
  35.8 1.1 fusion.5
  37.0 18.2 %all_to_all.40 = f32[32,4,128]{2,1,0:T(4,128)S(1)} all-to-all(f32[32,4,128]{2,1,0:T(4,128)S(1)} %broadcast_in_dim.31), channel_id=1, replica_groups=mesh['zh'=2,'x'=4,'y'=8,'zl'=4,'core'=2] {'x','y'}, dimensions={0} | all-to-all | bytes 131072 | tf_op jit(solution)/shard_map/all_to_all | solution.py:27
  55.2 0.6 multiply_reduce_fusion.4
  55.9 0.6 broadcast_in_dim.33
  56.5 3.4 %all-to-all-start.1 = ((f32[8,16,128]{2,1,0:T(8,128)}), f32[8,16,128]{2,1,0:T(8,128)S(1)}, u32[]{:S(2)}, u32[]{:S(2)}) async-start(f32[8,16,128]{2,1,0:T(8,128)} %broadcast_in_dim.33), calls=%async_computation.1 | async-start | bytes 131072 | tf_op jit(solution)/shard_map/all_to_all | solution.py:27
  59.9 8.2 %collective-permute-start.1 = (bf16[128,768]{1,0:T(8,128)(2,1)S(1)}, bf16[128,768]{1,0:T(8,128)(2,1)S(1)}, u32[]{:S(2)}, u32[]{:S(2)}) collective-permute-start(bf16[128,768]{1,0:T(8,128)(2,1)S(1)} %fusion.21), channel_id=1, source_target_pairs={{0,256},{256,0},{1,257},{257,1},{2,258},{258,2},{3,259},{259,3},{4... | collective-permute-start | bytes 589832 | tf_op jit(solution)/shard_map/ppermute | solution.py:20
  68.2 0.2 rev.9
  68.5 0.4 multiply_reduce_fusion.3
  69.0 0.6 broadcast_in_dim.35
  69.6 5.7 %all-to-all-start.2 = ((f32[32,4,128]{2,1,0:T(4,128)}), f32[32,4,128]{2,1,0:T(4,128)S(1)}, u32[]{:S(2)}, u32[]{:S(2)}) async-start(f32[32,4,128]{2,1,0:T(4,128)} %broadcast_in_dim.35), calls=%async_computation.2 | async-start | bytes 131072 | tf_op jit(solution)/shard_map/all_to_all | solution.py:27
  75.4 0.7 copy-done.4
  76.1 7.3 %all-to-all-done.2 = f32[32,4,128]{2,1,0:T(4,128)S(1)} async-done(((f32[32,4,128]{2,1,0:T(4,128)}), f32[32,4,128]{2,1,0:T(4,128)S(1)}, u32[]{:S(2)}, u32[]{:S(2)}) %all-to-all-start.2) | async-done | bytes 65568 | tf_op jit(solution)/shard_map/all_to_all | solution.py:27
  83.5 0.4 multiply_reduce_fusion.2
  83.9 10.6 %all_to_all.41 = f32[8,8,128]{2,1,0:T(8,128)S(1)} all-to-all(f32[8,8,128]{2,1,0:T(8,128)S(1)} %broadcast_in_dim.37), channel_id=1, replica_groups=mesh['zh'=2,'x'=4,'y'=8,'zl'=4,'core'=2] {'zl','core'}, dimensions={0} | all-to-all | bytes 65536 | tf_op jit(solution)/shard_map/all_to_all | solution.py:27
  94.5 0.1 rev.10
  94.7 0.4 multiply_reduce_fusion.1
  95.1 13.1 %all_to_all.42 = f32[32,4,128]{2,1,0:T(4,128)S(1)} all-to-all(f32[32,4,128]{2,1,0:T(4,128)S(1)} %broadcast_in_dim.77), channel_id=1, replica_groups=mesh['zh'=2,'x'=4,'y'=8,'zl'=4,'core'=2] {'x','y'}, dimensions={0} | all-to-all | bytes 131072 | tf_op jit(solution)/shard_map/all_to_all | solution.py:27
  108.3 0.4 multiply_reduce_fusion
  108.7 0.7 broadcast_in_dim.79
  109.4 3.5 %all-to-all-start.5 = ((f32[16,12,128]{2,1,0:T(8,128)}), f32[16,12,128]{2,1,0:T(8,128)S(1)}, u32[]{:S(2)}, u32[]{:S(2)}) async-start(f32[16,12,128]{2,1,0:T(8,128)} %broadcast_in_dim.79), calls=%async_computation.5 | async-start | bytes 262144 | tf_op jit(solution)/shard_map/all_to_all | solution.py:27
  112.9 9.0 %all-to-all-done.5 = f32[16,12,128]{2,1,0:T(8,128)S(1)} async-done(((f32[16,12,128]{2,1,0:T(8,128)}), f32[16,12,128]{2,1,0:T(8,128)S(1)}, u32[]{:S(2)}, u32[]{:S(2)}) %all-to-all-start.5) | async-done | bytes 98336 | tf_op jit(solution)/shard_map/all_to_all | solution.py:27
  122.0 0.1 rev.11
  122.2 1.5 constant_dynamic-slice_fusion.2
  123.7 1.5 multiply_convert_fusion
  125.3 1.5 convolution_convert_fusion.1
  126.9 2.3 %collective-permute-start.2 = (bf16[512,768]{1,0:T(8,128)(2,1)}, bf16[512,768]{1,0:T(8,128)(2,1)}, u32[]{:S(2)}, u32[]{:S(2)}) collective-permute-start(bf16[512,768]{1,0:T(8,128)(2,1)} %convolution_convert_fusion.1), channel_id=1, source_target_pairs={{0,1},{1,0},{2,3},{3,2},{4,5},{5,4},{6,7},{7,6},{8,9},{9,8},{10,11... | collective-permute-start | bytes 2359304 | tf_op jit(solution)/shard_map/ppermute | solution.py:20
  129.2 2.2 %convert_divide_fusion = (f32[768,512]{1,0:T(8,128)}, f32[512]{0:T(512)S(1)}, bf16[768,512]{1,0:T(8,128)(2,1)S(1)}) fusion(bf16[768,512]{1,0:T(8,128)(2,1)S(1)} %copy-done.1, f32[512]{0:T(512)S(1)} %add_sqrt_fusion, bf16[1024,768]{1,0:T(8,128)(2,1)S(1)} %copy-done.3, bf16[1024,512]{0,1:T(8,128)(2,1)S(1)} %multiply_convert_fusion), kind=kOutput, calls=%fused_computation.9 | convolution fusion | flops 807665152 | bytes 5771264 | tf_op jit(solution)/shard_map/dot_general | solution.py:113
  131.4 0.1 copy.19
  131.5 1.0 pad_maximum_fusion
  132.5 5.3 %all-to-all-start.6 = ((bf16[4,194,512]{2,1,0:T(8,128)(2,1)}), bf16[4,194,512]{2,1,0:T(8,128)(2,1)S(1)}, u32[]{:S(2)}, u32[]{:S(2)}) async-start(bf16[4,194,512]{2,1,0:T(8,128)(2,1)} %pad_maximum_fusion), calls=%async_computation.7 | async-start | bytes 1638400 | tf_op jit(solution)/shard_map/all_to_all | solution.py:123
  137.7 2.8 %add_convert_fusion = bf16[512,768]{1,0:T(8,128)(2,1)} fusion(bf16[512,768]{1,0:T(8,128)(2,1)} %collective-permute-done.2, bf16[1024,512]{0,1:T(8,128)(2,1)} %copy-done.5, f32[512]{0:T(512)S(1)} %add_sqrt_fusion, bf16[768,512]{1,0:T(8,128)(2,1)S(1)} %copy-done.1), kind=kOutput, calls=%fused_computation.18 | convolution fusion | flops 405798912 | bytes 2885632 | tf_op jit(solution)/shard_map/dot_general | solution.py:107
  140.6 8.2 %all-to-all-done.6 = bf16[4,194,512]{2,1,0:T(8,128)(2,1)S(1)} async-done(((bf16[4,194,512]{2,1,0:T(8,128)(2,1)}), bf16[4,194,512]{2,1,0:T(8,128)(2,1)S(1)}, u32[]{:S(2)}, u32[]{:S(2)}) %all-to-all-start.6) | async-done | bytes 794656 | tf_op jit(solution)/shard_map/all_to_all | solution.py:123
  148.8 0.1 convert_reduce_fusion
  149.1 0.8 pad_maximum_fusion.1
  149.8 7.8 %all-to-all-start.7 = ((bf16[16,14,512]{2,1,0:T(8,128)(2,1)}), bf16[16,14,512]{2,1,0:T(8,128)(2,1)S(1)}, u32[]{:S(2)}, u32[]{:S(2)}) async-start(bf16[16,14,512]{2,1,0:T(8,128)(2,1)} %pad_maximum_fusion.1), calls=%async_computation.8 | async-start | bytes 524288 | tf_op jit(solution)/shard_map/all_to_all | solution.py:127
  157.7 13.5 %all-to-all-done.7 = bf16[16,14,512]{2,1,0:T(8,128)(2,1)S(1)} async-done(((bf16[16,14,512]{2,1,0:T(8,128)(2,1)}), bf16[16,14,512]{2,1,0:T(8,128)(2,1)S(1)}, u32[]{:S(2)}, u32[]{:S(2)}) %all-to-all-start.7) | async-done | bytes 229408 | tf_op jit(solution)/shard_map/all_to_all | solution.py:127
  171.2 1.4 fusion.15
  172.7 2.4 %reduce-scatter.2.cloned.1.call-done = bf16[128,768]{1,0:T(8,128)(2,1)} async-done(((bf16[512,768]{1,0:T(8,128)(2,1)}), bf16[128,768]{1,0:T(8,128)(2,1)}) %reduce-scatter.2.cloned.1.call-update) | async-done | bytes 196624 | tf_op jit(solution)/shard_map/reduce_scatter | solution.py:111
  175.1 1.2 fusion.10
  176.2 1.8 fusion.14
  (67 shorter events, 0.9 us)
Async XLA Ops:
  7.2 26.4 %copy-start.1 = (bf16[768,512]{1,0:T(8,128)(2,1)S(1)}, bf16[768,512]{1,0:T(8,128)(2,1)}, u32[]{:S(2)}) copy-start(bf16[768,512]{1,0:T(8,128)(2,1)} %param.3) | copy-start | bytes 2359300
  31.6 4.2 %collective-permute-start = (bf16[512,768]{1,0:T(8,128)(2,1)S(1)}, bf16[512,768]{1,0:T(8,128)(2,1)S(1)}, u32[]{:S(2)}, u32[]{:S(2)}) collective-permute-start(bf16[512,768]{1,0:T(8,128)(2,1)S(1)} %all_gather.9), channel_id=1, source_target_pairs={{0,1},{1,0},{2,3},{3,2},{4,5},{5,4},{6,7},{7,6},{8,9},{9,8},{10,11... | collective-permute-start | bytes 2359304 | tf_op jit(solution)/shard_map/ppermute | solution.py:20
  35.8 1.2 copy-start.2
  56.5 11.6 %all-to-all-start.1 = ((f32[8,16,128]{2,1,0:T(8,128)}), f32[8,16,128]{2,1,0:T(8,128)S(1)}, u32[]{:S(2)}, u32[]{:S(2)}) async-start(f32[8,16,128]{2,1,0:T(8,128)} %broadcast_in_dim.33), calls=%async_computation.1 | async-start | bytes 131072 | tf_op jit(solution)/shard_map/all_to_all | solution.py:27
  59.9 15.5 %collective-permute-start.1 = (bf16[128,768]{1,0:T(8,128)(2,1)S(1)}, bf16[128,768]{1,0:T(8,128)(2,1)S(1)}, u32[]{:S(2)}, u32[]{:S(2)}) collective-permute-start(bf16[128,768]{1,0:T(8,128)(2,1)S(1)} %fusion.21), channel_id=1, source_target_pairs={{0,256},{256,0},{1,257},{257,1},{2,258},{258,2},{3,259},{259,3},{4... | collective-permute-start | bytes 589832 | tf_op jit(solution)/shard_map/ppermute | solution.py:20
  69.6 13.8 %all-to-all-start.2 = ((f32[32,4,128]{2,1,0:T(4,128)}), f32[32,4,128]{2,1,0:T(4,128)S(1)}, u32[]{:S(2)}, u32[]{:S(2)}) async-start(f32[32,4,128]{2,1,0:T(4,128)} %broadcast_in_dim.35), calls=%async_computation.2 | async-start | bytes 131072 | tf_op jit(solution)/shard_map/all_to_all | solution.py:27
  75.3 46.9 %all-gather.3.cloned.1.call-start = ((), (), s32[]{:S(2)}) async-start(), calls=%async_computation.10 | async-start | bytes 1769472 | tf_op jit(solution)/shard_map/all_gather | solution.py:66
  75.4 0.7 copy-start.4
  109.4 12.5 %all-to-all-start.5 = ((f32[16,12,128]{2,1,0:T(8,128)}), f32[16,12,128]{2,1,0:T(8,128)S(1)}, u32[]{:S(2)}, u32[]{:S(2)}) async-start(f32[16,12,128]{2,1,0:T(8,128)} %broadcast_in_dim.79), calls=%async_computation.5 | async-start | bytes 262144 | tf_op jit(solution)/shard_map/all_to_all | solution.py:27
  125.3 3.9 %copy-start.5 = (bf16[1024,512]{0,1:T(8,128)(2,1)}, bf16[1024,512]{0,1:T(8,128)(2,1)S(1)}, u32[]{:S(2)}) copy-start(bf16[1024,512]{0,1:T(8,128)(2,1)S(1)} %multiply_convert_fusion) | copy-start | bytes 3145732
  125.3 3.9 %copy-start.3 = (bf16[1024,768]{1,0:T(8,128)(2,1)S(1)}, bf16[1024,768]{1,0:T(8,128)(2,1)}, u32[]{:S(2)}) copy-start(bf16[1024,768]{1,0:T(8,128)(2,1)} %copy-done.2) | copy-start | bytes 4718596
  126.9 10.9 %collective-permute-start.2 = (bf16[512,768]{1,0:T(8,128)(2,1)}, bf16[512,768]{1,0:T(8,128)(2,1)}, u32[]{:S(2)}, u32[]{:S(2)}) collective-permute-start(bf16[512,768]{1,0:T(8,128)(2,1)} %convolution_convert_fusion.1), channel_id=1, source_target_pairs={{0,1},{1,0},{2,3},{3,2},{4,5},{5,4},{6,7},{7,6},{8,9},{9,8},{10,11... | collective-permute-start | bytes 2359304 | tf_op jit(solution)/shard_map/ppermute | solution.py:20
  132.5 16.3 %all-to-all-start.6 = ((bf16[4,194,512]{2,1,0:T(8,128)(2,1)}), bf16[4,194,512]{2,1,0:T(8,128)(2,1)S(1)}, u32[]{:S(2)}, u32[]{:S(2)}) async-start(bf16[4,194,512]{2,1,0:T(8,128)(2,1)} %pad_maximum_fusion), calls=%async_computation.7 | async-start | bytes 1638400 | tf_op jit(solution)/shard_map/all_to_all | solution.py:123
  137.7 37.3 %reduce-scatter.2.cloned.1.call-start = ((), (), s32[]{:S(2)}) async-start(), calls=%async_computation.9 | async-start | bytes 983040 | tf_op jit(solution)/shard_map/reduce_scatter | solution.py:111
  140.6 34.5 %copy-start = (bf16[1,128,768]{2,1,0:T(8,128)(2,1)S(1)}, bf16[1,128,768]{2,1,0:T(8,128)(2,1)}, u32[]{:S(2)}) copy-start(bf16[1,128,768]{2,1,0:T(8,128)(2,1)} %param.2) | copy-start | bytes 589828
  149.8 21.3 %all-to-all-start.7 = ((bf16[16,14,512]{2,1,0:T(8,128)(2,1)}), bf16[16,14,512]{2,1,0:T(8,128)(2,1)S(1)}, u32[]{:S(2)}, u32[]{:S(2)}) async-start(bf16[16,14,512]{2,1,0:T(8,128)(2,1)} %pad_maximum_fusion.1), calls=%async_computation.8 | async-start | bytes 524288 | tf_op jit(solution)/shard_map/all_to_all | solution.py:127
Sparse Core Ops, SparseCore 0:
  78.8 40.6 all-gather.2
  141.4 33.6 reduce-scatter.1

commit v3 on v2

v3 whole, which is shorter than its diff:
```python
import jax
import jax.numpy as jnp
from jax import lax
from jax.sharding import Mesh
from jax.sharding import PartitionSpec as P

SWEEPS = 3

sink_eps = 0.05
pred_temp = 0.1
grad_scale = 8.0

FINE = ("zh", "x", "y", "zl", "core")
DP = ("x", "y")
MP = ("zl", "core")
LANES = 128


def swapped(value, axis):
    return lax.ppermute(value, axis, [(0, 1), (1, 0)])


def shared(vector, axes):
    size = lax.axis_size(axes)
    tile = vector.reshape(1, -1, LANES)
    spread = jnp.broadcast_to(tile, (size,) + tile.shape[1:])
    return lax.all_to_all(spread, axes, 0, 0, tiled=True)


def high_low(vector, copies):
    high = vector.astype(jnp.bfloat16)
    low = (vector - high.astype(jnp.float32)).astype(jnp.bfloat16)
    return jnp.broadcast_to(jnp.stack([high, low])[None], (copies, 2) + vector.shape)


def on_device(views, prototypes):
    f32, bf16 = jnp.float32, jnp.bfloat16
    inputs = views[0].astype(f32)
    row_norm = jnp.sqrt(jnp.sum(inputs * inputs, axis=-1, keepdims=True) + 1e-06)
    unit_rows = inputs / row_norm
    unit_half = unit_rows.astype(bf16)
    weights = prototypes.astype(f32)
    proto_norm = jnp.sqrt(jnp.sum(weights * weights, axis=0, keepdims=True) + 1e-06)
    columns = weights / proto_norm
    columns_half = columns.astype(bf16)

    width = unit_half.shape[1]
    protos = columns_half.shape[1]
    partner_half = swapped(unit_half, "zh")
    core = lax.axis_index("core")
    zh = lax.axis_index("zh")

    def interleaved(own, other):
        first, second = jnp.where(core == 0, own, other), jnp.where(core == 0, other, own)
        return jnp.stack([first, second], axis=1).reshape(-1, width)

    line = lax.all_gather(unit_half, "zl", axis=0, tiled=False)
    grouped = interleaved(line, swapped(line, "core"))
    group_rows = grouped.shape[0]

    to_scores = (((0,), (1,)), ((), ()))
    scores = lax.dot_general(columns_half, grouped, to_scores, preferred_element_type=f32)
    expos = jnp.exp(scores / sink_eps)
    expo_pred = jnp.exp(scores / pred_temp)
    partner_group = lax.all_gather(partner_half, MP, axis=0, tiled=True)

    row_scale = None
    for sweep in range(SWEEPS):
        weighted = expos if row_scale is None else expos * row_scale[None, :]
        pieces = shared(jnp.sum(weighted, axis=1), DP)
        col_scale = 1.0 / jnp.sum(pieces, axis=0).reshape(protos)
        partial = jnp.sum(expos * col_scale[:, None], axis=0)
        if sweep == 0:
            both = jnp.concatenate([partial, jnp.sum(expo_pred, axis=0)])
            totals = jnp.sum(shared(both, MP), axis=0).reshape(2, group_rows)
            row_scale = 1.0 / totals[0]
            pred_scale = 1.0 / totals[1]
        elif sweep < SWEEPS - 1:
            row_scale = 1.0 / jnp.sum(shared(partial, MP), axis=0).reshape(group_rows)
        else:
            sent = jnp.concatenate([partial, col_scale, pred_scale])
            pieces = shared(sent, ("zh",) + MP).reshape(2, lax.axis_size(MP), -1)
            row_scales = 1.0 / jnp.sum(pieces[:, :, :group_rows], axis=1)
            row_scale = jnp.where(zh == 0, row_scales[0], row_scales[1])
            partner_rows = jnp.where(zh == 0, row_scales[1], row_scales[0])
            pieces = lax.dynamic_index_in_dim(pieces, 1 - zh, 0, keepdims=False)
            pieces = lax.dynamic_index_in_dim(pieces, lax.axis_index(MP), 0, keepdims=False)
            partner_cols = pieces[group_rows : group_rows + protos]
            partner_pred = pieces[group_rows + protos :]

    def grads(own_scores, own_pred, code_scores, code_cols, code_rows):
        predicted = jnp.exp(own_scores / pred_temp) * own_pred[None, :]
        codes = (jnp.exp(code_scores / sink_eps) * code_cols[:, None] * code_rows[None, :]).astype(bf16)
        return (grad_scale * (predicted - codes.astype(f32)) / pred_temp).astype(bf16)

    def mine(array):
        return lax.dynamic_slice_in_dim(array, zh * (protos // 2), protos // 2, 0)

    partner_scores = lax.dot_general(columns_half, partner_group, to_scores, preferred_element_type=f32)
    grad_half = grads(scores, pred_scale, partner_scores, partner_cols, partner_rows)
    partner_grad = grads(mine(partner_scores), partner_pred, mine(scores), mine(col_scale), row_scale)

    page_part = lax.dot_general(grad_half, columns_half, to_scores, preferred_element_type=f32).astype(bf16)
    page_grad = lax.psum_scatter(page_part, MP, scatter_dimension=0, tiled=True).astype(f32)

    by_pages = (((0,), (1,)), ((), ()))
    column_part = lax.dot_general(
        grouped, mine(grad_half), by_pages, preferred_element_type=f32
    ) + lax.dot_general(partner_group, partner_grad, by_pages, preferred_element_type=f32)
    n_zh, n_x, n_y = lax.axis_size("zh"), lax.axis_size("x"), lax.axis_size("y")
    share = width // (n_zh * n_x * n_y)
    half = protos // 2
    column_sent = column_part.astype(bf16)
    inner_part = jnp.sum(lax.dynamic_slice_in_dim(columns, zh * half, half, 1) * column_sent.astype(f32), axis=0)
    parcels = column_sent.reshape(n_zh, n_x, n_y * share, half).transpose(1, 0, 2, 3)
    parcels = parcels.reshape(n_x, n_zh * n_y * share, half)
    parcels = jnp.concatenate([parcels, high_low(inner_part, n_x)], axis=1)
    summed = jnp.sum(lax.all_to_all(parcels, "x", 0, 0, tiled=True).astype(f32), axis=0)
    column_sent, inner_part = summed[: n_zh * n_y * share], jnp.sum(summed[n_zh * n_y * share :], axis=0)
    parcels = column_sent.astype(bf16).reshape(n_zh * n_y, share, half)
    parcels = jnp.concatenate([parcels, high_low(inner_part, n_zh * n_y)], axis=1)
    arrived = lax.all_to_all(parcels, ("zh", "y"), 0, 0, tiled=True).astype(f32)
    summed = jnp.sum(arrived.reshape(n_zh, n_y, share + 2, half), axis=1)
    summed = jnp.concatenate([summed[0], summed[1]], axis=1)
    column_grad = summed[:share]
    inner_cols = jnp.sum(summed[share:], axis=0, keepdims=True)
    start = lax.axis_index(("zh",) + DP) * share
    own_columns = lax.dynamic_slice_in_dim(columns, start, share, 0)
    proto_grad = (column_grad - own_columns * inner_cols) / proto_norm

    inner = jnp.sum(unit_rows * page_grad, axis=-1, keepdims=True)
    view_grad = ((page_grad - unit_rows * inner) / row_norm).astype(bf16)[None]
    return (view_grad, proto_grad)


def solution(mesh):
    fine = Mesh(mesh.devices.reshape(2, 4, 8, 4, 2), FINE)
    return jax.shard_map(
        on_device,
        mesh=fine,
        in_specs=(P("zh", DP + MP, None), P(None, MP)),
        out_specs=(P("zh", DP + MP, None), P(("zh",) + DP, MP)),
        check_vma=False,
    )
```

time: 186 us -> 181 us (0.973)
  waiting for transfers between devices: 42.4 us -> 30 us
  blocking collectives: 64.1 us -> 73.4 us
  starting transfers between devices: 38.2 us -> 33.4 us
    all_to_all x0 -> x1, blocking collectives: none -> 11.8 us  [on_device(): lax.all_to_all(parcels, 'x', 0, 0, tiled=True).astype(f32)]
    all_to_all x2 -> x1, starting transfers between devices: 13.1 us -> 3.51 us  [on_device(): arrived = lax.all_to_all(parcels, ('zh', 'y'), 0, 0, tiled=True).astype(f32)]
    all_to_all x2 -> x1, waiting for transfers between devices: 21.7 us -> 12.8 us  [on_device(): arrived = lax.all_to_all(parcels, ('zh', 'y'), 0, 0, tiled=True).astype(f32)]
    all_to_all x3, starting transfers between devices: 12.6 us -> 19.7 us  [shared(): return lax.all_to_all(spread, axes, 0, 0, tiled=True)]
    all_to_all x3, waiting for transfers between devices: 16.3 us -> 13.3 us  [shared(): return lax.all_to_all(spread, axes, 0, 0, tiled=True)]
    unnamed x15 -> x18, local copies, waits for them, and re-layouts: 0.75 us -> 3.33 us
    all_to_all x3, blocking collectives: 41.9 us -> 39.4 us  [shared(): return lax.all_to_all(spread, axes, 0, 0, tiled=True)]
    reduce_scatter x1, waiting for transfers between devices: 2.41 us -> 0.03 us  [on_device(): lax.psum_scatter(page_part, MP, scatter_dimension=0, tiled=True).astype(f32)]
  transfers between devices with their start and end apart: 10 -> 8, of which waited for: 6 -> 5; matrix products, arithmetic and copies ran while one was open for 7% -> 6% of each run, Pallas kernels for 0% -> 0%
where the time goes in v3:
time: 181 us; the launch traced here: 179 us
  blocking collectives  73.4 us (41%)
  starting transfers between devices  33.4 us (18%)
  waiting for transfers between devices  30 us (17%)
  between operations  14.5 us (8%)
  other arithmetic  11.8 us (7%)
  matrix products  10.6 us (6%)
  local copies, waits for them, and re-layouts  5.69 us (3%)
    all_to_all x3, blocking collectives, shared(): return lax.all_to_all(spread, axes, 0, 0, tiled=True)  39.4 us
    all_gather x1, blocking collectives, on_device(): line = lax.all_gather(unit_half, 'zl', axis=0, tiled=False)  22.2 us
    all_to_all x3, starting transfers between devices, shared(): return lax.all_to_all(spread, axes, 0, 0, tiled=True)  19.7 us
    all_to_all x3, waiting for transfers between devices, shared(): return lax.all_to_all(spread, axes, 0, 0, tiled=True)  13.3 us
    all_to_all x1, waiting for transfers between devices, on_device(): arrived = lax.all_to_all(parcels, ('zh', 'y'), 0, 0, tiled=True).astype(f32)  12.8 us
    all_to_all x1, blocking collectives, on_device(): lax.all_to_all(parcels, 'x', 0, 0, tiled=True).astype(f32)  11.8 us
    ppermute x2, starting transfers between devices, swapped(): return lax.ppermute(value, axis, [(0, 1), (1, 0)])  10.1 us
    dot_general x1, matrix products, on_device(): lax.dot_general(columns_half, partner_group, to_scores, preferred_element...  4.26 us
  transfers between devices with their start and end apart: 8, of which 5 were waited for; matrix products, arithmetic and copies ran while one was open for 6% of the time, Pallas kernels for 0%

profile of v3, /device:TPU:6, one launch (start us, length us, event | category | flops | bytes accessed | tf_op | source)
XLA Modules:
  0.0 179.4 jit_solution(14342267854077911662)
XLA Ops:
  7.2 1.1 fusion.16
  8.3 1.0 fusion.17
  9.3 22.2 %all_gather.7 = bf16[4,128,768]{2,1,0:T(8,128)(2,1)S(1)} all-gather(bf16[1,128,768]{2,1,0:T(8,128)(2,1)S(1)} %fusion.17), channel_id=1, replica_groups=mesh['zh'=2,'x'=4,'y'=8,'zl'=4,'core'=2] {'zl'}, dimensions={0}, use_global_device_ids=true | all-gather | bytes 983040 | tf_op jit(solution)/shard_map/all_gather | solution.py:57
  31.6 1.9 %collective-permute-start = (bf16[4,128,768]{2,1,0:T(8,128)(2,1)S(1)}, bf16[4,128,768]{2,1,0:T(8,128)(2,1)}, u32[]{:S(2)}, u32[]{:S(2)}) collective-permute-start(bf16[4,128,768]{2,1,0:T(8,128)(2,1)S(1)} %all_gather.7), channel_id=1, source_target_pairs={{0,1},{1,0},{2,3},{3,2},{4,5},{5,4},{6,7},{7,6},{8,9},{9,8},{10,11... | collective-permute-start | bytes 2359304 | tf_op jit(solution)/shard_map/ppermute | solution.py:20
  33.5 0.2 fusion.1
  33.7 2.1 %collective-permute-done = bf16[4,128,768]{2,1,0:T(8,128)(2,1)} collective-permute-done((bf16[4,128,768]{2,1,0:T(8,128)(2,1)S(1)}, bf16[4,128,768]{2,1,0:T(8,128)(2,1)}, u32[]{:S(2)}, u32[]{:S(2)}) %collective-permute-start) | collective-permute-done | bytes 786464 | tf_op jit(solution)/shard_map/ppermute | solution.py:20
  35.9 1.2 select_bitcast_fusion.1
  37.1 0.1 pad_maximum_fusion
  37.3 1.2 fusion.2
  38.5 0.6 broadcast_in_dim.29
  39.1 10.2 %all-to-all-start = ((f32[32,4,128]{2,1,0:T(4,128)}), f32[32,4,128]{2,1,0:T(4,128)S(1)}, u32[]{:S(2)}, u32[]{:S(2)}) async-start(f32[32,4,128]{2,1,0:T(4,128)} %broadcast_in_dim.29), calls=%async_computation | async-start | bytes 131072 | tf_op jit(solution)/shard_map/all_to_all | solution.py:27
  49.4 0.1 fusion.36
  49.5 8.2 %collective-permute-start.1 = (bf16[128,768]{1,0:T(8,128)(2,1)S(1)}, bf16[128,768]{1,0:T(8,128)(2,1)S(1)}, u32[]{:S(2)}, u32[]{:S(2)}) collective-permute-start(bf16[128,768]{1,0:T(8,128)(2,1)S(1)} %fusion.36), channel_id=1, source_target_pairs={{0,256},{256,0},{1,257},{257,1},{2,258},{258,2},{3,259},{259,3},{4... | collective-permute-start | bytes 589832 | tf_op jit(solution)/shard_map/ppermute | solution.py:20
  57.8 0.6 multiply_reduce_fusion.4
  58.4 0.6 broadcast_in_dim.30
  59.1 3.4 %all-to-all-start.1 = ((f32[8,16,128]{2,1,0:T(8,128)}), f32[8,16,128]{2,1,0:T(8,128)S(1)}, u32[]{:S(2)}, u32[]{:S(2)}) async-start(f32[8,16,128]{2,1,0:T(8,128)} %broadcast_in_dim.30), calls=%async_computation.1 | async-start | bytes 131072 | tf_op jit(solution)/shard_map/all_to_all | solution.py:27
  62.5 1.7 collective-permute-done.1
  64.1 0.7 copy-done.7
  64.8 3.4 %all-to-all-done.1 = f32[8,16,128]{2,1,0:T(8,128)S(1)} async-done(((f32[8,16,128]{2,1,0:T(8,128)}), f32[8,16,128]{2,1,0:T(8,128)S(1)}, u32[]{:S(2)}, u32[]{:S(2)}) %all-to-all-start.1) | async-done | bytes 65568 | tf_op jit(solution)/shard_map/all_to_all | solution.py:27
  68.3 0.4 multiply_reduce_fusion.3
  68.7 17.7 %all_to_all.40 = f32[32,4,128]{2,1,0:T(4,128)S(1)} all-to-all(f32[32,4,128]{2,1,0:T(4,128)S(1)} %broadcast_in_dim.32), channel_id=1, replica_groups=mesh['zh'=2,'x'=4,'y'=8,'zl'=4,'core'=2] {'x','y'}, dimensions={0} | all-to-all | bytes 131072 | tf_op jit(solution)/shard_map/all_to_all | solution.py:27
  86.5 0.4 multiply_reduce_fusion.2
  86.9 8.5 %all_to_all.41 = f32[8,8,128]{2,1,0:T(8,128)S(1)} all-to-all(f32[8,8,128]{2,1,0:T(8,128)S(1)} %broadcast_in_dim.34), channel_id=1, replica_groups=mesh['zh'=2,'x'=4,'y'=8,'zl'=4,'core'=2] {'zl','core'}, dimensions={0} | all-to-all | bytes 65536 | tf_op jit(solution)/shard_map/all_to_all | solution.py:27
  95.4 0.4 multiply_reduce_fusion.1
  95.9 13.1 %all_to_all.42 = f32[32,4,128]{2,1,0:T(4,128)S(1)} all-to-all(f32[32,4,128]{2,1,0:T(4,128)S(1)} %broadcast_in_dim.36), channel_id=1, replica_groups=mesh['zh'=2,'x'=4,'y'=8,'zl'=4,'core'=2] {'x','y'}, dimensions={0} | all-to-all | bytes 131072 | tf_op jit(solution)/shard_map/all_to_all | solution.py:27
  109.0 0.4 multiply_reduce_fusion
  109.4 0.7 broadcast_in_dim.38
  110.1 6.1 %all-to-all-start.5 = ((f32[16,20,128]{2,1,0:T(8,128)}), f32[16,20,128]{2,1,0:T(8,128)S(1)}, u32[]{:S(2)}, u32[]{:S(2)}) async-start(f32[16,20,128]{2,1,0:T(8,128)} %broadcast_in_dim.38), calls=%async_computation.5 | async-start | bytes 393216 | tf_op jit(solution)/shard_map/all_to_all | solution.py:27
  116.2 0.0 reduce-scatter.2.cloned.1.call-start
  116.3 9.9 %all-to-all-done.5 = f32[16,20,128]{2,1,0:T(8,128)S(1)} async-done(((f32[16,20,128]{2,1,0:T(8,128)}), f32[16,20,128]{2,1,0:T(8,128)S(1)}, u32[]{:S(2)}, u32[]{:S(2)}) %all-to-all-start.5) | async-done | bytes 163872 | tf_op jit(solution)/shard_map/all_to_all | solution.py:27
  126.2 0.1 dynamic-slice.2
  126.4 4.3 %multiply_convert_fusion = (bf16[512,1024]{1,0:T(8,128)(2,1)S(1)}, f32[512,1024]{1,0:T(8,128)}) fusion(f32[512,1024]{1,0:T(8,128)S(1)} %get-tuple-element.13, f32[1024]{0:T(1024)S(1)} %bitcast.80, f32[512]{0:T(512)S(1)} %bitcast.82, f32[1024]{0:T(1024)S(1)} %get-tuple-element.11, bf16[1024,768]{1,0:T(8,128)(2,1)} %all-gather.2.cloned.1.call-done, ...), kind=kOutput, calls=%fused_computation | convolution fusion | flops 811728896 | bytes 7614464 | tf_op jit(solution)/shard_map/dot_general | solution.py:99
  130.7 1.1 copy-done.5
  131.7 2.2 %convolution_convert_fusion = bf16[1024,768]{1,0:T(8,128)(2,1)} fusion(bf16[512,1024]{1,0:T(8,128)(2,1)S(1)} %get-tuple-element.14, bf16[768,512]{1,0:T(8,128)(2,1)S(1)} %copy-done.4, f32[512]{0:T(512)S(1)} %add_sqrt_fusion), kind=kOutput, calls=%fused_computation.12 | convolution fusion | flops 807272448 | bytes 3409920 | tf_op jit(solution)/shard_map/dot_general | solution.py:103
  134.0 0.2 convert_divide_fusion
  134.2 0.1 dynamic_slice.28
  134.3 0.1 dynamic-slice.3
  134.4 1.6 copy-done.8
  136.0 2.3 %fusion.3 = f32[768,256]{1,0:T(8,128)S(1)} fusion(bf16[1024,768]{1,0:T(8,128)(2,1)S(1)} %copy-done.8, f32[512,1024]{1,0:T(8,128)} %get-tuple-element.15, s32[]{:T(128)S(6)} %select_n.57, f32[512,1024]{1,0:T(8,128)S(1)} %get-tuple-element.13, f32[1024]{0:T(1024)S(1)} %bitcast.79, f32[256]{0:T(256)S(1)} %dynamic_slice.28, f32[1024]{0:T(1024)S(1)} %bitcast.78), kind=kOutput, calls=%fused_computation.23 | convolution fusion | flops 405274624 | bytes 4465668 | tf_op jit(solution)/shard_map/dot_general | solution.py:109
  138.2 0.6 multiply_reduce_fusion.5
  139.0 11.8 %all_to_all.43 = bf16[4,194,256]{2,1,0:T(8,128)(2,1)S(1)} all-to-all(bf16[4,194,256]{2,1,0:T(8,128)(2,1)S(1)} %pad_maximum_fusion.1), channel_id=1, replica_groups=mesh['zh'=2,'x'=4,'y'=8,'zl'=4,'core'=2] {'x'}, dimensions={0} | all-to-all | bytes 794624 | tf_op jit(solution)/shard_map/all_to_all | solution.py:118
  150.9 0.1 convert_reduce_fusion
  151.0 0.7 pad_maximum_fusion.2
  151.7 3.5 %all-to-all-start.7 = ((bf16[16,14,256]{2,1,0:T(8,128)(2,1)}), bf16[16,14,256]{2,1,0:T(8,128)(2,1)S(1)}, u32[]{:S(2)}, u32[]{:S(2)}) async-start(bf16[16,14,256]{2,1,0:T(8,128)(2,1)} %pad_maximum_fusion.2), calls=%async_computation.8 | async-start | bytes 262144 | tf_op jit(solution)/shard_map/all_to_all | solution.py:122
  155.3 12.8 %all-to-all-done.7 = bf16[16,14,256]{2,1,0:T(8,128)(2,1)S(1)} async-done(((bf16[16,14,256]{2,1,0:T(8,128)(2,1)}), bf16[16,14,256]{2,1,0:T(8,128)(2,1)S(1)}, u32[]{:S(2)}, u32[]{:S(2)}) %all-to-all-start.7) | async-done | bytes 114720 | tf_op jit(solution)/shard_map/all_to_all | solution.py:122
  168.1 1.4 fusion.22
  169.6 1.1 fusion.18
  170.7 1.8 fusion.21
  (58 shorter events, 0.7 us)
Async XLA Ops:
  7.2 26.3 %copy-start.4 = (bf16[768,512]{1,0:T(8,128)(2,1)S(1)}, bf16[768,512]{1,0:T(8,128)(2,1)}, u32[]{:S(2)}) copy-start(bf16[768,512]{1,0:T(8,128)(2,1)} %param.3) | copy-start | bytes 2359300
  31.6 4.3 %collective-permute-start = (bf16[4,128,768]{2,1,0:T(8,128)(2,1)S(1)}, bf16[4,128,768]{2,1,0:T(8,128)(2,1)}, u32[]{:S(2)}, u32[]{:S(2)}) collective-permute-start(bf16[4,128,768]{2,1,0:T(8,128)(2,1)S(1)} %all_gather.7), channel_id=1, source_target_pairs={{0,1},{1,0},{2,3},{3,2},{4,5},{5,4},{6,7},{7,6},{8,9},{9,8},{10,11... | collective-permute-start | bytes 2359304 | tf_op jit(solution)/shard_map/ppermute | solution.py:20
  37.3 1.2 copy-start
  37.3 12.1 %copy-start.2 = (bf16[1,128,768]{2,1,0:T(8,128)(2,1)S(1)}, bf16[1,128,768]{2,1,0:T(8,128)(2,1)}, u32[]{:S(2)}) copy-start(bf16[1,128,768]{2,1,0:T(8,128)(2,1)} %param.2) | copy-start | bytes 589828
  39.1 18.6 %all-to-all-start = ((f32[32,4,128]{2,1,0:T(4,128)}), f32[32,4,128]{2,1,0:T(4,128)S(1)}, u32[]{:S(2)}, u32[]{:S(2)}) async-start(f32[32,4,128]{2,1,0:T(4,128)} %broadcast_in_dim.29), calls=%async_computation | async-start | bytes 131072 | tf_op jit(solution)/shard_map/all_to_all | solution.py:27
  49.5 14.6 %collective-permute-start.1 = (bf16[128,768]{1,0:T(8,128)(2,1)S(1)}, bf16[128,768]{1,0:T(8,128)(2,1)S(1)}, u32[]{:S(2)}, u32[]{:S(2)}) collective-permute-start(bf16[128,768]{1,0:T(8,128)(2,1)S(1)} %fusion.36), channel_id=1, source_target_pairs={{0,256},{256,0},{1,257},{257,1},{2,258},{258,2},{3,259},{259,3},{4... | collective-permute-start | bytes 589832 | tf_op jit(solution)/shard_map/ppermute | solution.py:20
  59.1 9.2 %all-to-all-start.1 = ((f32[8,16,128]{2,1,0:T(8,128)}), f32[8,16,128]{2,1,0:T(8,128)S(1)}, u32[]{:S(2)}, u32[]{:S(2)}) async-start(f32[8,16,128]{2,1,0:T(8,128)} %broadcast_in_dim.30), calls=%async_computation.1 | async-start | bytes 131072 | tf_op jit(solution)/shard_map/all_to_all | solution.py:27
  62.4 64.0 %all-gather.2.cloned.1.call-start = ((), (), s32[]{:S(2)}) async-start(), calls=%async_computation.9 | async-start | bytes 1769472 | tf_op jit(solution)/shard_map/all_gather | solution.py:65
  64.1 0.7 copy-start.7
  110.1 16.1 %all-to-all-start.5 = ((f32[16,20,128]{2,1,0:T(8,128)}), f32[16,20,128]{2,1,0:T(8,128)S(1)}, u32[]{:S(2)}, u32[]{:S(2)}) async-start(f32[16,20,128]{2,1,0:T(8,128)} %broadcast_in_dim.38), calls=%async_computation.5 | async-start | bytes 393216 | tf_op jit(solution)/shard_map/all_to_all | solution.py:27
  116.2 53.4 %reduce-scatter.2.cloned.1.call-start = ((), (), s32[]{:S(2)}) async-start(), calls=%async_computation.10 | async-start | bytes 1769472 | tf_op jit(solution)/shard_map/reduce_scatter | solution.py:104
  130.7 1.1 copy-start.5
  134.0 2.0 %copy-start.8 = (bf16[1024,768]{1,0:T(8,128)(2,1)S(1)}, bf16[1024,768]{1,0:T(8,128)(2,1)}, u32[]{:S(2)}) copy-start(bf16[1024,768]{1,0:T(8,128)(2,1)} %all-gather.2.cloned.1.call-done) | copy-start | bytes 4718596
  134.2 4.0 %copy-start.3 = (f32[768,512]{1,0:T(8,128)}, f32[768,512]{1,0:T(8,128)S(1)}, u32[]{:S(2)}) copy-start(f32[768,512]{1,0:T(8,128)S(1)} %convert_divide_fusion) | copy-start | bytes 4718596
  136.0 2.3 %copy-start.1 = (bf16[4,2,128,768]{3,2,1,0:T(8,128)(2,1)S(1)}, bf16[4,2,128,768]{3,2,1,0:T(8,128)(2,1)}, u32[]{:S(2)}) copy-start(bf16[4,2,128,768]{3,2,1,0:T(8,128)(2,1)} %copy-done) | copy-start | bytes 4718596
  136.0 2.3 %copy-start.6 = (bf16[512,1024]{1,0:T(8,128)(2,1)S(1)}, bf16[512,1024]{1,0:T(8,128)(2,1)}, u32[]{:S(2)}) copy-start(bf16[512,1024]{1,0:T(8,128)(2,1)} %copy-done.5) | copy-start | bytes 3145732
  151.7 16.3 %all-to-all-start.7 = ((bf16[16,14,256]{2,1,0:T(8,128)(2,1)}), bf16[16,14,256]{2,1,0:T(8,128)(2,1)S(1)}, u32[]{:S(2)}, u32[]{:S(2)}) async-start(bf16[16,14,256]{2,1,0:T(8,128)(2,1)} %pad_maximum_fusion.2), calls=%async_computation.8 | async-start | bytes 262144 | tf_op jit(solution)/shard_map/all_to_all | solution.py:122
Sparse Core Ops, SparseCore 0:
  65.3 43.0 all-gather.1
  134.1 35.4 reduce-scatter.1

commit v4 on v3

--- a/solution.py
+++ b/solution.py
@@ -1,6 +1,8 @@
 import jax
 import jax.numpy as jnp
 from jax import lax
+from jax.experimental import pallas as pl
+from jax.experimental.pallas import tpu as pltpu
 from jax.sharding import Mesh
 from jax.sharding import PartitionSpec as P
 
@@ -33,12 +35,30 @@
     return jnp.broadcast_to(jnp.stack([high, low])[None], (copies, 2) + vector.shape)
 
 
-def on_device(views, prototypes):
-    f32, bf16 = jnp.float32, jnp.bfloat16
+def view_grad_kernel(views, page_grad, out):
+    f32 = jnp.float32
     inputs = views[0].astype(f32)
     row_norm = jnp.sqrt(jnp.sum(inputs * inputs, axis=-1, keepdims=True) + 1e-06)
     unit_rows = inputs / row_norm
-    unit_half = unit_rows.astype(bf16)
+    page = page_grad[...].astype(f32)
+    inner = jnp.sum(unit_rows * page, axis=-1, keepdims=True)
+    out[0] = ((page - unit_rows * inner) / row_norm).astype(out.dtype)
+
+
+def unit_kernel(views, out):
+    inputs = views[0].astype(jnp.float32)
+    row_norm = jnp.sqrt(jnp.sum(inputs * inputs, axis=-1, keepdims=True) + 1e-06)
+    out[...] = (inputs / row_norm).astype(out.dtype)
+
+
+def on_device(views, prototypes):
+    f32, bf16 = jnp.float32, jnp.bfloat16
+    unit_half = pl.pallas_call(
+        unit_kernel,
+        out_shape=jax.ShapeDtypeStruct(views.shape[1:], bf16),
+        compiler_params=pltpu.CompilerParams(vmem_limit_bytes=4 * 2**20),
+        name="unit_rows",
+    )(views)
     weights = prototypes.astype(f32)
     proto_norm = jnp.sqrt(jnp.sum(weights * weights, axis=0, keepdims=True) + 1e-06)
     columns = weights / proto_norm
@@ -51,10 +71,11 @@
     zh = lax.axis_index("zh")
 
     def interleaved(own, other):
+        blocks = (-1, 1) + unit_half.shape
         first, second = jnp.where(core == 0, own, other), jnp.where(core == 0, other, own)
-        return jnp.stack([first, second], axis=1).reshape(-1, width)
+        return jnp.concatenate([first.reshape(blocks), second.reshape(blocks)], axis=1).reshape(-1, width)
 
-    line = lax.all_gather(unit_half, "zl", axis=0, tiled=False)
+    line = lax.all_gather(unit_half, "zl", axis=0, tiled=True)
     grouped = interleaved(line, swapped(line, "core"))
     group_rows = grouped.shape[0]
 
@@ -79,7 +100,7 @@
             row_scale = 1.0 / jnp.sum(shared(partial, MP), axis=0).reshape(group_rows)
         else:
             sent = jnp.concatenate([partial, col_scale, pred_scale])
-            pieces = shared(sent, ("zh",) + MP).reshape(2, lax.axis_size(MP), -1)
+            pieces = shared(sent.astype(bf16), ("zh",) + MP).astype(f32).reshape(2, lax.axis_size(MP), -1)
             row_scales = 1.0 / jnp.sum(pieces[:, :, :group_rows], axis=1)
             row_scale = jnp.where(zh == 0, row_scales[0], row_scales[1])
             partner_rows = jnp.where(zh == 0, row_scales[1], row_scales[0])
@@ -96,17 +117,22 @@
     def mine(array):
         return lax.dynamic_slice_in_dim(array, zh * (protos // 2), protos // 2, 0)
 
+    my_columns = lax.dynamic_slice_in_dim(columns_half, zh * (protos // 2), protos // 2, 1)
+
     partner_scores = lax.dot_general(columns_half, partner_group, to_scores, preferred_element_type=f32)
     grad_half = grads(scores, pred_scale, partner_scores, partner_cols, partner_rows)
-    partner_grad = grads(mine(partner_scores), partner_pred, mine(scores), mine(col_scale), row_scale)
+    page_part = lax.dot_general(grad_half, columns_half, to_scores, preferred_element_type=f32).astype(bf16)
+    page_grad = lax.psum_scatter(page_part, MP, scatter_dimension=0, tiled=True)
 
-    page_part = lax.dot_general(grad_half, columns_half, to_scores, preferred_element_type=f32).astype(bf16)
-    page_grad = lax.psum_scatter(page_part, MP, scatter_dimension=0, tiled=True).astype(f32)
-
+    my_scores = mine(scores)
+    my_partner = lax.dot_general(my_columns, partner_group, to_scores, preferred_element_type=f32)
+    my_grad = grads(my_scores, pred_scale, my_partner, mine(partner_cols), partner_rows)
+    partner_grad = grads(my_partner, partner_pred, my_scores, mine(col_scale), row_scale)
     by_pages = (((0,), (1,)), ((), ()))
     column_part = lax.dot_general(
-        grouped, mine(grad_half), by_pages, preferred_element_type=f32
+        grouped, my_grad, by_pages, preferred_element_type=f32
     ) + lax.dot_general(partner_group, partner_grad, by_pages, preferred_element_type=f32)
+
     n_zh, n_x, n_y = lax.axis_size("zh"), lax.axis_size("x"), lax.axis_size("y")
     share = width // (n_zh * n_x * n_y)
     half = protos // 2
@@ -128,8 +154,12 @@
     own_columns = lax.dynamic_slice_in_dim(columns, start, share, 0)
     proto_grad = (column_grad - own_columns * inner_cols) / proto_norm
 
-    inner = jnp.sum(unit_rows * page_grad, axis=-1, keepdims=True)
-    view_grad = ((page_grad - unit_rows * inner) / row_norm).astype(bf16)[None]
+    view_grad = pl.pallas_call(
+        view_grad_kernel,
+        out_shape=jax.ShapeDtypeStruct(views.shape, views.dtype),
+        compiler_params=pltpu.CompilerParams(vmem_limit_bytes=4 * 2**20),
+        name="view_grad",
+    )(views, page_grad)
     return (view_grad, proto_grad)
 
 

time: 181 us -> 176 us (0.972)
  waiting for transfers between devices: 30 us -> 26 us
  other arithmetic: 11.8 us -> 8.99 us
    dot_general x1, matrix products: 2.24 us -> 5.01 us  [on_device(): lax.dot_general(grad_half, columns_half, to_scores, preferred_element_typ...]
    reduce_sum x2 -> x0, other arithmetic: 2.27 us -> none  [the longest x1 1.15 us: on_device(): inner = jnp.sum(unit_rows * page_grad, axis=-1, keepdims=True)]
    all_to_all x3, waiting for transfers between devices: 13.3 us -> 11.2 us  [shared(): return lax.all_to_all(spread, axes, 0, 0, tiled=True)]
    dot_general x2, matrix products: 4.91 us -> 3.04 us  [the longest x1 2.15 us: on_device(): lax.dot_general(my_columns, partner_group, to_scores, preferred_element_t...]
  transfers between devices with their start and end apart: 8 -> 8, of which waited for: 5 -> 4; matrix products, arithmetic and copies ran while one was open for 6% -> 8% of each run, Pallas kernels for 0% -> 0%
where the time goes in v4:
time: 176 us; the launch traced here: 174 us
  blocking collectives  73.7 us (42%)
  starting transfers between devices  33.4 us (19%)
  waiting for transfers between devices  26 us (15%)
  between operations  14.4 us (8%)
  matrix products  10.2 us (6%)
  other arithmetic  8.99 us (5%)
  local copies, waits for them, and re-layouts  5.8 us (3%)
    all_to_all x3, blocking collectives, shared(): return lax.all_to_all(spread, axes, 0, 0, tiled=True)  39.7 us
    all_gather x1, blocking collectives, on_device(): line = lax.all_gather(unit_half, 'zl', axis=0, tiled=True)  22.4 us
    all_to_all x3, starting transfers between devices, shared(): return lax.all_to_all(spread, axes, 0, 0, tiled=True)  19.7 us
    all_to_all x1, waiting for transfers between devices, on_device(): arrived = lax.all_to_all(parcels, ('zh', 'y'), 0, 0, tiled=True).astype(f32)  12.7 us
    all_to_all x1, blocking collectives, on_device(): lax.all_to_all(parcels, 'x', 0, 0, tiled=True).astype(f32)  11.7 us
    all_to_all x3, waiting for transfers between devices, shared(): return lax.all_to_all(spread, axes, 0, 0, tiled=True)  11.2 us
    ppermute x2, starting transfers between devices, swapped(): return lax.ppermute(value, axis, [(0, 1), (1, 0)])  10.1 us
    dot_general x1, matrix products, on_device(): lax.dot_general(grad_half, columns_half, to_scores, preferred_element_typ...  5.01 us
  transfers between devices with their start and end apart: 8, of which 4 were waited for; matrix products, arithmetic and copies ran while one was open for 8% of the time, Pallas kernels for 0%

profile of v4, /device:TPU:6, one launch (start us, length us, event | category | flops | bytes accessed | tf_op | source)
XLA Modules:
  0.0 173.6 jit_solution(13510689662218034552)
XLA Ops:
  7.2 0.9 copy-done
  8.1 0.1 unit_rows.1
  8.2 22.4 %all_gather.6 = bf16[512,768]{1,0:T(8,128)(2,1)S(1)} all-gather(bf16[128,768]{1,0:T(8,128)(2,1)S(1)} %unit_rows.1), channel_id=1, replica_groups=mesh['zh'=2,'x'=4,'y'=8,'zl'=4,'core'=2] {'zl'}, dimensions={0}, use_global_device_ids=true | all-gather | bytes 983040 | tf_op jit(solution)/shard_map/all_gather | solution.py:78
  30.6 1.9 %collective-permute-start = (bf16[512,768]{1,0:T(8,128)(2,1)S(1)}, bf16[512,768]{1,0:T(8,128)(2,1)}, u32[]{:S(2)}, u32[]{:S(2)}) collective-permute-start(bf16[512,768]{1,0:T(8,128)(2,1)S(1)} %all_gather.6), channel_id=1, source_target_pairs={{0,1},{1,0},{2,3},{3,2},{4,5},{5,4},{6,7},{7,6},{8,9},{9,8},{10,11... | collective-permute-start | bytes 2359304 | tf_op jit(solution)/shard_map/ppermute | solution.py:22
  32.5 1.3 fusion.1
  33.9 1.4 convert_divide_fusion
  35.3 1.2 broadcast_select_fusion.1
  36.6 0.1 pad_maximum_fusion
  36.7 1.1 fusion.2
  37.9 0.6 broadcast_in_dim.25
  38.5 10.2 %all-to-all-start = ((f32[32,4,128]{2,1,0:T(4,128)}), f32[32,4,128]{2,1,0:T(4,128)S(1)}, u32[]{:S(2)}, u32[]{:S(2)}) async-start(f32[32,4,128]{2,1,0:T(4,128)} %broadcast_in_dim.25), calls=%async_computation | async-start | bytes 131072 | tf_op jit(solution)/shard_map/all_to_all | solution.py:29
  48.8 8.2 %collective-permute-start.1 = (bf16[128,768]{1,0:T(8,128)(2,1)S(1)}, bf16[128,768]{1,0:T(8,128)(2,1)S(1)}, u32[]{:S(2)}, u32[]{:S(2)}) collective-permute-start(bf16[128,768]{1,0:T(8,128)(2,1)S(1)} %unit_rows.1), channel_id=1, source_target_pairs={{0,256},{256,0},{1,257},{257,1},{2,258},{258,2},{3,259},{259,3},{4... | collective-permute-start | bytes 589832 | tf_op jit(solution)/shard_map/ppermute | solution.py:22
  57.1 0.6 multiply_reduce_fusion.4
  57.7 0.6 broadcast_in_dim.26
  58.3 3.3 %all-to-all-start.1 = ((f32[8,16,128]{2,1,0:T(8,128)}), f32[8,16,128]{2,1,0:T(8,128)S(1)}, u32[]{:S(2)}, u32[]{:S(2)}) async-start(f32[8,16,128]{2,1,0:T(8,128)} %broadcast_in_dim.26), calls=%async_computation.1 | async-start | bytes 131072 | tf_op jit(solution)/shard_map/all_to_all | solution.py:29
  61.8 2.0 %collective-permute-done.1 = bf16[128,768]{1,0:T(8,128)(2,1)S(1)} collective-permute-done((bf16[128,768]{1,0:T(8,128)(2,1)S(1)}, bf16[128,768]{1,0:T(8,128)(2,1)S(1)}, u32[]{:S(2)}, u32[]{:S(2)}) %collective-permute-start.1) | collective-permute-done | bytes 196640 | tf_op jit(solution)/shard_map/ppermute | solution.py:22
  63.8 0.7 copy-done.8
  64.5 3.1 %all-to-all-done.1 = f32[8,16,128]{2,1,0:T(8,128)S(1)} async-done(((f32[8,16,128]{2,1,0:T(8,128)}), f32[8,16,128]{2,1,0:T(8,128)S(1)}, u32[]{:S(2)}, u32[]{:S(2)}) %all-to-all-start.1) | async-done | bytes 65568 | tf_op jit(solution)/shard_map/all_to_all | solution.py:29
  67.6 0.4 multiply_reduce_fusion.3
  68.0 17.7 %all_to_all.40 = f32[32,4,128]{2,1,0:T(4,128)S(1)} all-to-all(f32[32,4,128]{2,1,0:T(4,128)S(1)} %broadcast_in_dim.28), channel_id=1, replica_groups=mesh['zh'=2,'x'=4,'y'=8,'zl'=4,'core'=2] {'x','y'}, dimensions={0} | all-to-all | bytes 131072 | tf_op jit(solution)/shard_map/all_to_all | solution.py:29
  85.8 0.4 multiply_reduce_fusion.2
  86.2 8.9 %all_to_all.41 = f32[8,8,128]{2,1,0:T(8,128)S(1)} all-to-all(f32[8,8,128]{2,1,0:T(8,128)S(1)} %broadcast_in_dim.30), channel_id=1, replica_groups=mesh['zh'=2,'x'=4,'y'=8,'zl'=4,'core'=2] {'zl','core'}, dimensions={0} | all-to-all | bytes 65536 | tf_op jit(solution)/shard_map/all_to_all | solution.py:29
  95.1 0.4 multiply_reduce_fusion.1
  95.5 13.1 %all_to_all.42 = f32[32,4,128]{2,1,0:T(4,128)S(1)} all-to-all(f32[32,4,128]{2,1,0:T(4,128)S(1)} %broadcast_in_dim.32), channel_id=1, replica_groups=mesh['zh'=2,'x'=4,'y'=8,'zl'=4,'core'=2] {'x','y'}, dimensions={0} | all-to-all | bytes 131072 | tf_op jit(solution)/shard_map/all_to_all | solution.py:29
  108.7 0.4 multiply_reduce_fusion
  109.1 0.6 broadcast_in_dim.33
  109.8 6.1 %all-to-all-start.5 = ((bf16[16,20,128]{2,1,0:T(8,128)(2,1)}), bf16[16,20,128]{2,1,0:T(8,128)(2,1)S(1)}, u32[]{:S(2)}, u32[]{:S(2)}) async-start(bf16[16,20,128]{2,1,0:T(8,128)(2,1)} %broadcast_in_dim.33), calls=%async_computation.5 | async-start | bytes 196608 | tf_op jit(solution)/shard_map/all_to_all | solution.py:29
  115.8 0.0 reduce-scatter.2.cloned.1.call-start
  115.9 0.1 dynamic_slice.28
  116.0 8.2 %all-to-all-done.5 = bf16[16,20,128]{2,1,0:T(8,128)(2,1)S(1)} async-done(((bf16[16,20,128]{2,1,0:T(8,128)(2,1)}), bf16[16,20,128]{2,1,0:T(8,128)(2,1)S(1)}, u32[]{:S(2)}, u32[]{:S(2)}) %all-to-all-start.5) | async-done | bytes 81952 | tf_op jit(solution)/shard_map/all_to_all | solution.py:29
  124.2 0.1 reshape.176
  124.2 0.1 dynamic-slice.3
  124.3 0.1 dynamic-slice.5
  124.4 0.1 dynamic-slice.4
  124.6 5.0 %convolution_convert_fusion = bf16[1024,768]{1,0:T(8,128)(2,1)} fusion(bf16[768,512]{1,0:T(8,128)(2,1)S(1)} %get-tuple-element.9, f32[512,1024]{1,0:T(8,128)S(1)} %get-tuple-element.18, bf16[1024,768]{1,0:T(8,128)(2,1)} %all-gather.2.cloned.1.call-done, f32[1024]{0:T(1024)S(1)} %bitcast.74, f32[512]{0:T(512)S(1)} %bitcast.78, f32[1024]{0:T(1024)S(1)} %get-tuple-element.14), kind=kOutput, calls=%fused_computation.12 | convolution fusion | flops 1616642048 | bytes 6039552 | tf_op jit(solution)/shard_map/dot_general | solution.py:124
  129.6 2.1 %fusion.16 = f32[256,1024]{1,0:T(8,128)S(1)} fusion(bf16[1024,768]{1,0:T(8,128)(2,1)} %all-gather.2.cloned.1.call-done, bf16[768,512]{1,0:T(8,128)(2,1)S(1)} %get-tuple-element.9, s32[]{:T(128)S(6)} %select_n.57), kind=kOutput, calls=%fused_computation.40 | convolution fusion | flops 402653184 | bytes 3014660 | tf_op jit(solution)/shard_map/dot_general | solution.py:128
  131.8 1.0 convolution_bitcast_fusion
  132.8 0.4 copy-done.4
  133.2 0.5 copy-done.6
  133.6 0.9 multiply_reduce_fusion.5
  134.7 11.7 %all_to_all.43 = bf16[4,194,256]{2,1,0:T(8,128)(2,1)S(1)} all-to-all(bf16[4,194,256]{2,1,0:T(8,128)(2,1)S(1)} %pad_maximum_fusion.1), channel_id=1, replica_groups=mesh['zh'=2,'x'=4,'y'=8,'zl'=4,'core'=2] {'x'}, dimensions={0} | all-to-all | bytes 794624 | tf_op jit(solution)/shard_map/all_to_all | solution.py:144
  146.3 0.1 convert_reduce_fusion
  146.5 0.7 pad_maximum_fusion.2
  147.2 3.5 %all-to-all-start.7 = ((bf16[16,14,256]{2,1,0:T(8,128)(2,1)}), bf16[16,14,256]{2,1,0:T(8,128)(2,1)S(1)}, u32[]{:S(2)}, u32[]{:S(2)}) async-start(bf16[16,14,256]{2,1,0:T(8,128)(2,1)} %pad_maximum_fusion.2), calls=%async_computation.8 | async-start | bytes 262144 | tf_op jit(solution)/shard_map/all_to_all | solution.py:148
  150.7 12.7 %all-to-all-done.7 = bf16[16,14,256]{2,1,0:T(8,128)(2,1)S(1)} async-done(((bf16[16,14,256]{2,1,0:T(8,128)(2,1)}), bf16[16,14,256]{2,1,0:T(8,128)(2,1)S(1)}, u32[]{:S(2)}, u32[]{:S(2)}) %all-to-all-start.7) | async-done | bytes 114720 | tf_op jit(solution)/shard_map/all_to_all | solution.py:148
  163.5 1.4 fusion.18
  164.9 0.9 copy-done.2
  165.9 0.9 view_grad.1
  (55 shorter events, 0.6 us)
Async XLA Ops:
  7.2 0.9 copy-start
  8.1 25.8 %copy-start.3 = (bf16[768,512]{1,0:T(8,128)(2,1)S(1)}, bf16[768,512]{1,0:T(8,128)(2,1)}, u32[]{:S(2)}) copy-start(bf16[768,512]{1,0:T(8,128)(2,1)} %param.3) | copy-start | bytes 2359300
  30.6 4.7 %collective-permute-start = (bf16[512,768]{1,0:T(8,128)(2,1)S(1)}, bf16[512,768]{1,0:T(8,128)(2,1)}, u32[]{:S(2)}, u32[]{:S(2)}) collective-permute-start(bf16[512,768]{1,0:T(8,128)(2,1)S(1)} %all_gather.6), channel_id=1, source_target_pairs={{0,1},{1,0},{2,3},{3,2},{4,5},{5,4},{6,7},{7,6},{8,9},{9,8},{10,11... | collective-permute-start | bytes 2359304 | tf_op jit(solution)/shard_map/ppermute | solution.py:22
  36.7 1.2 copy-start.5
  38.5 18.5 %all-to-all-start = ((f32[32,4,128]{2,1,0:T(4,128)}), f32[32,4,128]{2,1,0:T(4,128)S(1)}, u32[]{:S(2)}, u32[]{:S(2)}) async-start(f32[32,4,128]{2,1,0:T(4,128)} %broadcast_in_dim.25), calls=%async_computation | async-start | bytes 131072 | tf_op jit(solution)/shard_map/all_to_all | solution.py:29
  48.8 15.0 %collective-permute-start.1 = (bf16[128,768]{1,0:T(8,128)(2,1)S(1)}, bf16[128,768]{1,0:T(8,128)(2,1)S(1)}, u32[]{:S(2)}, u32[]{:S(2)}) collective-permute-start(bf16[128,768]{1,0:T(8,128)(2,1)S(1)} %unit_rows.1), channel_id=1, source_target_pairs={{0,256},{256,0},{1,257},{257,1},{2,258},{258,2},{3,259},{259,3},{4... | collective-permute-start | bytes 589832 | tf_op jit(solution)/shard_map/ppermute | solution.py:22
  58.3 9.2 %all-to-all-start.1 = ((f32[8,16,128]{2,1,0:T(8,128)}), f32[8,16,128]{2,1,0:T(8,128)S(1)}, u32[]{:S(2)}, u32[]{:S(2)}) async-start(f32[8,16,128]{2,1,0:T(8,128)} %broadcast_in_dim.26), calls=%async_computation.1 | async-start | bytes 131072 | tf_op jit(solution)/shard_map/all_to_all | solution.py:29
  61.7 62.8 %all-gather.2.cloned.1.call-start = ((), (), s32[]{:S(2)}) async-start(), calls=%async_computation.9 | async-start | bytes 1769472 | tf_op jit(solution)/shard_map/all_gather | solution.py:86
  63.8 0.7 copy-start.8
  109.8 14.4 %all-to-all-start.5 = ((bf16[16,20,128]{2,1,0:T(8,128)(2,1)}), bf16[16,20,128]{2,1,0:T(8,128)(2,1)S(1)}, u32[]{:S(2)}, u32[]{:S(2)}) async-start(bf16[16,20,128]{2,1,0:T(8,128)(2,1)} %broadcast_in_dim.33), calls=%async_computation.5 | async-start | bytes 196608 | tf_op jit(solution)/shard_map/all_to_all | solution.py:29
  115.8 49.1 %reduce-scatter.2.cloned.1.call-start = ((), (), s32[]{:S(2)}) async-start(), calls=%async_computation.10 | async-start | bytes 1769472 | tf_op jit(solution)/shard_map/reduce_scatter | solution.py:125
  129.6 2.2 %copy-start.7 = (bf16[1024,768]{1,0:T(8,128)(2,1)S(1)}, bf16[1024,768]{1,0:T(8,128)(2,1)}, u32[]{:S(2)}) copy-start(bf16[1024,768]{1,0:T(8,128)(2,1)} %all-gather.2.cloned.1.call-done) | copy-start | bytes 4718596
  131.8 1.4 copy-start.4
  131.8 1.9 %copy-start.6 = (bf16[4,2,128,768]{3,2,1,0:T(8,128)(2,1)S(1)}, bf16[4,2,128,768]{3,2,1,0:T(8,128)(2,1)}, u32[]{:S(2)}) copy-start(bf16[4,2,128,768]{3,2,1,0:T(8,128)(2,1)} %copy-done.5) | copy-start | bytes 4718596
  134.6 30.4 %copy-start.1 = (bf16[1,128,768]{2,1,0:T(8,128)(2,1)S(1)}, bf16[1,128,768]{2,1,0:T(8,128)(2,1)}, u32[]{:S(2)}) copy-start(bf16[1,128,768]{2,1,0:T(8,128)(2,1)} %views.3) | copy-start | bytes 589828
  147.2 16.2 %all-to-all-start.7 = ((bf16[16,14,256]{2,1,0:T(8,128)(2,1)}), bf16[16,14,256]{2,1,0:T(8,128)(2,1)S(1)}, u32[]{:S(2)}, u32[]{:S(2)}) async-start(bf16[16,14,256]{2,1,0:T(8,128)(2,1)} %pad_maximum_fusion.2), calls=%async_computation.8 | async-start | bytes 262144 | tf_op jit(solution)/shard_map/all_to_all | solution.py:148
  164.9 0.9 copy-start.2
Sparse Core Ops, SparseCore 0:
  65.2 42.8 all-gather.1
  129.7 34.9 reduce-scatter.1

commit v5 on v4

--- a/solution.py
+++ b/solution.py
@@ -22,17 +22,11 @@
     return lax.ppermute(value, axis, [(0, 1), (1, 0)])
 
 
-def shared(vector, axes):
+def shared(vector, axes, kind=jnp.bfloat16):
     size = lax.axis_size(axes)
-    tile = vector.reshape(1, -1, LANES)
+    tile = vector.astype(kind).reshape(1, -1, LANES)
     spread = jnp.broadcast_to(tile, (size,) + tile.shape[1:])
-    return lax.all_to_all(spread, axes, 0, 0, tiled=True)
-
-
-def high_low(vector, copies):
-    high = vector.astype(jnp.bfloat16)
-    low = (vector - high.astype(jnp.float32)).astype(jnp.bfloat16)
-    return jnp.broadcast_to(jnp.stack([high, low])[None], (copies, 2) + vector.shape)
+    return lax.all_to_all(spread, axes, 0, 0, tiled=True).astype(jnp.float32)
 
 
 def view_grad_kernel(views, page_grad, out):
@@ -70,15 +64,13 @@
     core = lax.axis_index("core")
     zh = lax.axis_index("zh")
 
-    def interleaved(own, other):
-        blocks = (-1, 1) + unit_half.shape
-        first, second = jnp.where(core == 0, own, other), jnp.where(core == 0, other, own)
-        return jnp.concatenate([first.reshape(blocks), second.reshape(blocks)], axis=1).reshape(-1, width)
-
-    line = lax.all_gather(unit_half, "zl", axis=0, tiled=True)
-    grouped = interleaved(line, swapped(line, "core"))
+    line = lax.all_gather(unit_half, "zl", axis=0, tiled=False)
+    other = swapped(line, "core")
+    by_chip = jnp.zeros(line.shape[:1] + (2,) + line.shape[1:], bf16)
+    by_chip = lax.dynamic_update_index_in_dim(by_chip, line, core, 1)
+    by_chip = lax.dynamic_update_index_in_dim(by_chip, other, 1 - core, 1)
+    grouped = by_chip.reshape(-1, width)
     group_rows = grouped.shape[0]
-
     to_scores = (((0,), (1,)), ((), ()))
     scores = lax.dot_general(columns_half, grouped, to_scores, preferred_element_type=f32)
     expos = jnp.exp(scores / sink_eps)
@@ -88,7 +80,7 @@
     row_scale = None
     for sweep in range(SWEEPS):
         weighted = expos if row_scale is None else expos * row_scale[None, :]
-        pieces = shared(jnp.sum(weighted, axis=1), DP)
+        pieces = shared(jnp.sum(weighted, axis=1), DP, f32)
         col_scale = 1.0 / jnp.sum(pieces, axis=0).reshape(protos)
         partial = jnp.sum(expos * col_scale[:, None], axis=0)
         if sweep == 0:
@@ -100,7 +92,7 @@
             row_scale = 1.0 / jnp.sum(shared(partial, MP), axis=0).reshape(group_rows)
         else:
             sent = jnp.concatenate([partial, col_scale, pred_scale])
-            pieces = shared(sent.astype(bf16), ("zh",) + MP).astype(f32).reshape(2, lax.axis_size(MP), -1)
+            pieces = shared(sent, ("zh",) + MP).reshape(2, lax.axis_size(MP), -1)
             row_scales = 1.0 / jnp.sum(pieces[:, :, :group_rows], axis=1)
             row_scale = jnp.where(zh == 0, row_scales[0], row_scales[1])
             partner_rows = jnp.where(zh == 0, row_scales[1], row_scales[0])
@@ -136,23 +128,16 @@
     n_zh, n_x, n_y = lax.axis_size("zh"), lax.axis_size("x"), lax.axis_size("y")
     share = width // (n_zh * n_x * n_y)
     half = protos // 2
-    column_sent = column_part.astype(bf16)
-    inner_part = jnp.sum(lax.dynamic_slice_in_dim(columns, zh * half, half, 1) * column_sent.astype(f32), axis=0)
+    exact = lax.dynamic_slice_in_dim(columns, zh * half, half, 1)
+    inner = jnp.sum(exact * column_part, axis=0, keepdims=True)
+    column_sent = (column_part - exact * inner).astype(bf16)
     parcels = column_sent.reshape(n_zh, n_x, n_y * share, half).transpose(1, 0, 2, 3)
     parcels = parcels.reshape(n_x, n_zh * n_y * share, half)
-    parcels = jnp.concatenate([parcels, high_low(inner_part, n_x)], axis=1)
     summed = jnp.sum(lax.all_to_all(parcels, "x", 0, 0, tiled=True).astype(f32), axis=0)
-    column_sent, inner_part = summed[: n_zh * n_y * share], jnp.sum(summed[n_zh * n_y * share :], axis=0)
-    parcels = column_sent.astype(bf16).reshape(n_zh * n_y, share, half)
-    parcels = jnp.concatenate([parcels, high_low(inner_part, n_zh * n_y)], axis=1)
+    parcels = summed.astype(bf16).reshape(n_zh * n_y, share, half)
     arrived = lax.all_to_all(parcels, ("zh", "y"), 0, 0, tiled=True).astype(f32)
-    summed = jnp.sum(arrived.reshape(n_zh, n_y, share + 2, half), axis=1)
-    summed = jnp.concatenate([summed[0], summed[1]], axis=1)
-    column_grad = summed[:share]
-    inner_cols = jnp.sum(summed[share:], axis=0, keepdims=True)
-    start = lax.axis_index(("zh",) + DP) * share
-    own_columns = lax.dynamic_slice_in_dim(columns, start, share, 0)
-    proto_grad = (column_grad - own_columns * inner_cols) / proto_norm
+    summed = jnp.sum(arrived.reshape(n_zh, n_y, share, half), axis=1)
+    proto_grad = jnp.concatenate([summed[0], summed[1]], axis=1) / proto_norm
 
     view_grad = pl.pallas_call(
         view_grad_kernel,

time: 176 us -> 173 us (0.983)
  blocking collectives: 73.7 us -> 88.2 us
  waiting for transfers between devices: 26 us -> 16.2 us
  other arithmetic: 8.99 us -> 5.07 us
  starting transfers between devices: 33.4 us -> 30.1 us
    all_to_all x3 -> x4, blocking collectives: 39.7 us -> 54.3 us  [the longest x3 38.9 us: shared(): return lax.all_to_all(spread, axes, 0, 0, tiled=True).astype(jnp.float32)]
    all_to_all x4 -> x3, waiting for transfers between devices: 23.9 us -> 11.3 us  [shared(): return lax.all_to_all(spread, axes, 0, 0, tiled=True).astype(jnp.float32)]
    all_to_all x4 -> x3, starting transfers between devices: 23.2 us -> 19.7 us  [shared(): return lax.all_to_all(spread, axes, 0, 0, tiled=True).astype(jnp.float32)]
    reduce_scatter x1, waiting for transfers between devices: 0.01 us -> 2.62 us  [on_device(): page_grad = lax.psum_scatter(page_part, MP, scatter_dimension=0, tiled=True)]
  transfers between devices with their start and end apart: 8 -> 7, of which waited for: 4 -> 5; matrix products, arithmetic and copies ran while one was open for 8% -> 6% of each run, Pallas kernels for 0% -> 0%
where the time goes in v5:
time: 173 us; the launch traced here: 172 us
  blocking collectives  88.2 us (51%)
  starting transfers between devices  30.1 us (17%)
  waiting for transfers between devices  16.2 us (9%)
  between operations  14.4 us (8%)
  matrix products  10.2 us (6%)
  local copies, waits for them, and re-layouts  7.12 us (4%)
  other arithmetic  5.07 us (3%)
    all_to_all x3, blocking collectives, shared(): return lax.all_to_all(spread, axes, 0, 0, tiled=True).astype(jnp.float32)  38.9 us
    all_gather x1, blocking collectives, on_device(): line = lax.all_gather(unit_half, 'zl', axis=0, tiled=False)  22.4 us
    all_to_all x3, starting transfers between devices, shared(): return lax.all_to_all(spread, axes, 0, 0, tiled=True).astype(jnp.float32)  19.7 us
    all_to_all x1, blocking collectives, on_device(): arrived = lax.all_to_all(parcels, ('zh', 'y'), 0, 0, tiled=True).astype(f32)  15.3 us
    all_to_all x1, blocking collectives, on_device(): lax.all_to_all(parcels, 'x', 0, 0, tiled=True).astype(f32)  11.6 us
    all_to_all x3, waiting for transfers between devices, shared(): return lax.all_to_all(spread, axes, 0, 0, tiled=True).astype(jnp.float32)  11.3 us
    ppermute x2, starting transfers between devices, swapped(): return lax.ppermute(value, axis, [(0, 1), (1, 0)])  10.1 us
    dot_general x1, matrix products, on_device(): lax.dot_general(grad_half, columns_half, to_scores, preferred_element_typ...  5 us
  transfers between devices with their start and end apart: 7, of which 5 were waited for; matrix products, arithmetic and copies ran while one was open for 6% of the time, Pallas kernels for 0%

profile of v5, /device:TPU:6, one launch (start us, length us, event | category | flops | bytes accessed | tf_op | source)
XLA Modules:
  0.0 172.2 jit_solution(5274622715424790951)
XLA Ops:
  7.2 0.9 copy-done
  8.1 0.1 unit_rows.1
  8.2 22.4 %all-gather = bf16[512,768]{1,0:T(8,128)(2,1)S(1)} all-gather(bf16[128,768]{1,0:T(8,128)(2,1)S(1)} %unit_rows.1), channel_id=2, replica_groups=mesh['zh'=2,'x'=4,'y'=8,'zl'=4,'core'=2] {'zl'}, dimensions={0}, use_global_device_ids=true | all-gather | bytes 983040 | tf_op jit(solution)/shard_map/all_gather | solution.py:67
  30.6 1.9 %collective-permute-start = (bf16[4,128,768]{2,1,0:T(8,128)(2,1)S(1)}, bf16[4,128,768]{2,1,0:T(8,128)(2,1)}, u32[]{:S(2)}, u32[]{:S(2)}) collective-permute-start(bf16[4,128,768]{2,1,0:T(8,128)(2,1)S(1)} %bitcast.64), channel_id=1, source_target_pairs={{0,1},{1,0},{2,3},{3,2},{4,5},{5,4},{6,7},{7,6},{8,9},{9,8},{10,11... | collective-permute-start | bytes 2359304 | tf_op jit(solution)/shard_map/ppermute | solution.py:22
  32.5 0.1 broadcast_in_dim.27
  32.6 0.1 constant_dynamic-update-slice_fusion
  32.7 0.2 fusion.1
  33.0 1.4 convert_divide_fusion
  34.4 0.5 collective-permute-done
  34.9 1.2 bitcast_dynamic-update-slice_fusion
  36.1 1.1 fusion.2
  37.3 0.6 broadcast_in_dim.31
  37.9 10.2 %all-to-all-start = ((f32[32,4,128]{2,1,0:T(4,128)}), f32[32,4,128]{2,1,0:T(4,128)S(1)}, u32[]{:S(2)}, u32[]{:S(2)}) async-start(f32[32,4,128]{2,1,0:T(4,128)} %broadcast_in_dim.31), calls=%async_computation | async-start | bytes 131072 | tf_op jit(solution)/shard_map/all_to_all | solution.py:29
  48.2 8.2 %collective-permute-start.1 = (bf16[128,768]{1,0:T(8,128)(2,1)S(1)}, bf16[128,768]{1,0:T(8,128)(2,1)S(1)}, u32[]{:S(2)}, u32[]{:S(2)}) collective-permute-start(bf16[128,768]{1,0:T(8,128)(2,1)S(1)} %unit_rows.1), channel_id=1, source_target_pairs={{0,256},{256,0},{1,257},{257,1},{2,258},{258,2},{3,259},{259,3},{4... | collective-permute-start | bytes 589832 | tf_op jit(solution)/shard_map/ppermute | solution.py:22
  56.4 0.6 multiply_reduce_fusion.4
  57.1 0.6 broadcast_in_dim.32
  57.7 3.3 %all-to-all-start.1 = ((bf16[8,16,128]{2,1,0:T(8,128)(2,1)}), bf16[8,16,128]{2,1,0:T(8,128)(2,1)S(1)}, u32[]{:S(2)}, u32[]{:S(2)}) async-start(bf16[8,16,128]{2,1,0:T(8,128)(2,1)} %broadcast_in_dim.32), calls=%async_computation.1 | async-start | bytes 65536 | tf_op jit(solution)/shard_map/all_to_all | solution.py:29
  61.1 1.7 collective-permute-done.1
  62.8 0.7 copy-done.8
  63.5 3.2 %all-to-all-done.1 = bf16[8,16,128]{2,1,0:T(8,128)(2,1)S(1)} async-done(((bf16[8,16,128]{2,1,0:T(8,128)(2,1)}), bf16[8,16,128]{2,1,0:T(8,128)(2,1)S(1)}, u32[]{:S(2)}, u32[]{:S(2)}) %all-to-all-start.1) | async-done | bytes 32800 | tf_op jit(solution)/shard_map/all_to_all | solution.py:29
  66.8 0.4 multiply_reduce_fusion.3
  67.2 17.7 %all_to_all.40 = f32[32,4,128]{2,1,0:T(4,128)S(1)} all-to-all(f32[32,4,128]{2,1,0:T(4,128)S(1)} %broadcast_in_dim.34), channel_id=1, replica_groups=mesh['zh'=2,'x'=4,'y'=8,'zl'=4,'core'=2] {'x','y'}, dimensions={0} | all-to-all | bytes 131072 | tf_op jit(solution)/shard_map/all_to_all | solution.py:29
  85.0 0.4 multiply_reduce_fusion.2
  85.4 8.0 %all_to_all.41 = bf16[8,8,128]{2,1,0:T(8,128)(2,1)S(1)} all-to-all(bf16[8,8,128]{2,1,0:T(8,128)(2,1)S(1)} %broadcast_in_dim.35), channel_id=1, replica_groups=mesh['zh'=2,'x'=4,'y'=8,'zl'=4,'core'=2] {'zl','core'}, dimensions={0} | all-to-all | bytes 32768 | tf_op jit(solution)/shard_map/all_to_all | solution.py:29
  93.4 0.4 multiply_reduce_fusion.1
  93.9 13.2 %all_to_all.42 = f32[32,4,128]{2,1,0:T(4,128)S(1)} all-to-all(f32[32,4,128]{2,1,0:T(4,128)S(1)} %broadcast_in_dim.72), channel_id=1, replica_groups=mesh['zh'=2,'x'=4,'y'=8,'zl'=4,'core'=2] {'x','y'}, dimensions={0} | all-to-all | bytes 131072 | tf_op jit(solution)/shard_map/all_to_all | solution.py:29
  107.1 0.4 multiply_reduce_fusion
  107.5 0.6 broadcast_in_dim.73
  108.2 6.1 %all-to-all-start.5 = ((bf16[16,20,128]{2,1,0:T(8,128)(2,1)}), bf16[16,20,128]{2,1,0:T(8,128)(2,1)S(1)}, u32[]{:S(2)}, u32[]{:S(2)}) async-start(bf16[16,20,128]{2,1,0:T(8,128)(2,1)} %broadcast_in_dim.73), calls=%async_computation.5 | async-start | bytes 196608 | tf_op jit(solution)/shard_map/all_to_all | solution.py:29
  114.3 0.2 reduce-scatter.2.cloned.1.call-start
  114.5 8.1 %all-to-all-done.5 = bf16[16,20,128]{2,1,0:T(8,128)(2,1)S(1)} async-done(((bf16[16,20,128]{2,1,0:T(8,128)(2,1)}), bf16[16,20,128]{2,1,0:T(8,128)(2,1)S(1)}, u32[]{:S(2)}, u32[]{:S(2)}) %all-to-all-start.5) | async-done | bytes 81952 | tf_op jit(solution)/shard_map/all_to_all | solution.py:29
  122.7 0.1 dynamic-slice.3
  122.8 5.0 %convolution_convert_fusion = bf16[1024,768]{1,0:T(8,128)(2,1)} fusion(bf16[768,512]{1,0:T(8,128)(2,1)S(1)} %get-tuple-element.7, f32[512,1024]{1,0:T(8,128)S(1)} %get-tuple-element.16, bf16[1024,768]{1,0:T(8,128)(2,1)} %all-gather.3.cloned.1.call-done, f32[1024]{0:T(1024)S(1)} %bitcast.68, f32[512]{0:T(512)S(1)} %bitcast.79, f32[1024]{0:T(1024)S(1)} %get-tuple-element.12), kind=kOutput, calls=%fused_computation.12 | convolution fusion | flops 1616642048 | bytes 6039552 | tf_op jit(solution)/shard_map/dot_general | solution.py:116
  127.9 0.1 dynamic_slice.25
  128.0 0.1 dynamic-slice.4
  128.0 0.1 dynamic-slice.5
  128.1 2.2 %fusion.15 = f32[256,1024]{1,0:T(8,128)S(1)} fusion(bf16[1024,768]{1,0:T(8,128)(2,1)} %all-gather.3.cloned.1.call-done, bf16[768,512]{1,0:T(8,128)(2,1)S(1)} %get-tuple-element.7, s32[]{:T(128)S(6)} %select_n.48), kind=kOutput, calls=%fused_computation.36 | convolution fusion | flops 402653184 | bytes 3014660 | tf_op jit(solution)/shard_map/dot_general | solution.py:120
  130.3 1.0 convolution_bitcast_fusion
  131.3 0.4 copy-done.3
  131.7 0.5 copy-done.5
  132.2 0.9 multiply_reduce_fusion.5
  133.0 0.2 subtract_convert_fusion
  133.3 11.6 %all_to_all.43 = bf16[4,192,256]{2,1,0:T(8,128)(2,1)S(1)} all-to-all(bf16[4,192,256]{2,1,0:T(8,128)(2,1)S(1)} %bitcast.66), channel_id=1, replica_groups=mesh['zh'=2,'x'=4,'y'=8,'zl'=4,'core'=2] {'x'}, dimensions={0} | all-to-all | bytes 786432 | tf_op jit(solution)/shard_map/all_to_all | solution.py:136
  144.9 15.3 %all_to_all.44 = bf16[16,12,256]{2,1,0:T(8,128)(2,1)S(1)} all-to-all(bf16[16,12,256]{2,1,0:T(8,128)(2,1)S(1)} %reshape.139), channel_id=1, replica_groups=mesh['zh'=2,'x'=4,'y'=8,'zl'=4,'core'=2] {'zh','y'}, dimensions={0} | all-to-all | bytes 196608 | tf_op jit(solution)/shard_map/all_to_all | solution.py:138
  160.3 0.6 maximum_divide_fusion
  160.9 2.6 %reduce-scatter.2.cloned.1.call-done.page_grad = bf16[128,768]{1,0:T(8,128)(2,1)} async-done(((bf16[1024,768]{1,0:T(8,128)(2,1)}), bf16[128,768]{1,0:T(8,128)(2,1)}) %reduce-scatter.2.cloned.1.call-update) | async-done | bytes 196624 | tf_op jit(solution)/shard_map/reduce_scatter | solution.py:117
  163.6 0.9 copy-done.2
  164.5 0.9 view_grad.1
  (43 shorter events, 0.6 us)
Async XLA Ops:
  7.2 0.9 copy-start
  8.2 24.5 %copy-start.6 = (bf16[768,512]{1,0:T(8,128)(2,1)S(1)}, bf16[768,512]{1,0:T(8,128)(2,1)}, u32[]{:S(2)}) copy-start(bf16[768,512]{1,0:T(8,128)(2,1)} %param.3) | copy-start | bytes 2359300
  30.6 4.3 %collective-permute-start = (bf16[4,128,768]{2,1,0:T(8,128)(2,1)S(1)}, bf16[4,128,768]{2,1,0:T(8,128)(2,1)}, u32[]{:S(2)}, u32[]{:S(2)}) collective-permute-start(bf16[4,128,768]{2,1,0:T(8,128)(2,1)S(1)} %bitcast.64), channel_id=1, source_target_pairs={{0,1},{1,0},{2,3},{3,2},{4,5},{5,4},{6,7},{7,6},{8,9},{9,8},{10,11... | collective-permute-start | bytes 2359304 | tf_op jit(solution)/shard_map/ppermute | solution.py:22
  36.1 1.2 copy-start.4
  37.9 18.5 %all-to-all-start = ((f32[32,4,128]{2,1,0:T(4,128)}), f32[32,4,128]{2,1,0:T(4,128)S(1)}, u32[]{:S(2)}, u32[]{:S(2)}) async-start(f32[32,4,128]{2,1,0:T(4,128)} %broadcast_in_dim.31), calls=%async_computation | async-start | bytes 131072 | tf_op jit(solution)/shard_map/all_to_all | solution.py:29
  48.2 14.6 %collective-permute-start.1 = (bf16[128,768]{1,0:T(8,128)(2,1)S(1)}, bf16[128,768]{1,0:T(8,128)(2,1)S(1)}, u32[]{:S(2)}, u32[]{:S(2)}) collective-permute-start(bf16[128,768]{1,0:T(8,128)(2,1)S(1)} %unit_rows.1), channel_id=1, source_target_pairs={{0,256},{256,0},{1,257},{257,1},{2,258},{258,2},{3,259},{259,3},{4... | collective-permute-start | bytes 589832 | tf_op jit(solution)/shard_map/ppermute | solution.py:22
  57.7 9.0 %all-to-all-start.1 = ((bf16[8,16,128]{2,1,0:T(8,128)(2,1)}), bf16[8,16,128]{2,1,0:T(8,128)(2,1)S(1)}, u32[]{:S(2)}, u32[]{:S(2)}) async-start(bf16[8,16,128]{2,1,0:T(8,128)(2,1)} %broadcast_in_dim.32), calls=%async_computation.1 | async-start | bytes 65536 | tf_op jit(solution)/shard_map/all_to_all | solution.py:29
  61.1 61.8 %all-gather.3.cloned.1.call-start = ((), (), s32[]{:S(2)}) async-start(), calls=%async_computation.9 | async-start | bytes 1769472 | tf_op jit(solution)/shard_map/all_gather | solution.py:78
  62.8 0.7 copy-start.8
  108.2 14.4 %all-to-all-start.5 = ((bf16[16,20,128]{2,1,0:T(8,128)(2,1)}), bf16[16,20,128]{2,1,0:T(8,128)(2,1)S(1)}, u32[]{:S(2)}, u32[]{:S(2)}) async-start(bf16[16,20,128]{2,1,0:T(8,128)(2,1)} %broadcast_in_dim.73), calls=%async_computation.5 | async-start | bytes 196608 | tf_op jit(solution)/shard_map/all_to_all | solution.py:29
  114.3 49.3 %reduce-scatter.2.cloned.1.call-start = ((), (), s32[]{:S(2)}) async-start(), calls=%async_computation.10 | async-start | bytes 1769472 | tf_op jit(solution)/shard_map/reduce_scatter | solution.py:117
  127.9 2.4 %copy-start.7 = (bf16[1024,768]{1,0:T(8,128)(2,1)S(1)}, bf16[1024,768]{1,0:T(8,128)(2,1)}, u32[]{:S(2)}) copy-start(bf16[1024,768]{1,0:T(8,128)(2,1)} %all-gather.3.cloned.1.call-done) | copy-start | bytes 4718596
  130.3 1.4 copy-start.3
  130.3 1.9 %copy-start.5 = (bf16[4,2,128,768]{3,2,1,0:T(8,128)(2,1)S(1)}, bf16[4,2,128,768]{3,2,1,0:T(8,128)(2,1)}, u32[]{:S(2)}) copy-start(bf16[4,2,128,768]{3,2,1,0:T(8,128)(2,1)} %copy-done.4) | copy-start | bytes 4718596
  133.0 30.5 %copy-start.1 = (bf16[1,128,768]{2,1,0:T(8,128)(2,1)S(1)}, bf16[1,128,768]{2,1,0:T(8,128)(2,1)}, u32[]{:S(2)}) copy-start(bf16[1,128,768]{2,1,0:T(8,128)(2,1)} %views.3) | copy-start | bytes 589828
  163.5 0.9 copy-start.2
Sparse Core Ops, SparseCore 0:
  64.6 42.3 all-gather.2
  128.0 35.5 reduce-scatter.1
